TPU v7x, 128 devices: a whole 4x4x4 slice. The times are simulated.
128 devices in a mesh: chan: 32 (over z_hi, y, x), hel: 4 (over z_lo, core).
Axes of the slice: x: 4, y: 4, z: 4 (z_hi: 2, z_lo: 2; z = z_hi * 2 + z_lo), core: 2. Of those that a mesh axis runs over, the one named last changes fastest.
Arguments:
- psi_prev: float32 [12, 4096, 256], P('hel', 'chan'), may hold values from -6 to 6
- psi_cur: float32 [12, 4096, 256], P('hel', 'chan'), may hold values from -6 to 6
- blocks: bfloat16 [12, 32, 8, 8, 128, 128], P('hel', 'chan'), may hold values from -0.015625 to 0.015625
- radial_terms: float32 [8, 256], replicated, may hold values from -4 to 4
- energies: float32 [12, 4096], P('hel', 'chan'), may hold values from -0.6 to 0
- rotation: float32 [12, 4096], P('hel', 'chan'), may hold values from 0 to 1
- coriolis: float32 [12, 4096], P('hel', 'chan'), may hold values from 0.2 to 1
- counts: int32 [12], P('hel'), may hold values from 64 to 4096, as said below
- offsets: int32 [12, 7], P('hel'), may hold values from 1 to 31, as said below
Outputs:
- psi_before: float32 [12, 4096, 256], P('hel', 'chan')
- psi_last: float32 [12, 4096, 256], P('hel', 'chan')
Inputs may be any that keep to these rules, and one draw needn't show every extreme that they name: `counts`: counts never rise with helicity; helicity 0 has all 4096 channels and the last helicity has 64. Each row holds 7 distinct offsets; its first three are 1, 16 and 31.
All inputs are finite; a program needn't handle non-finite values.
Results may differ from a plain program's by a relative error of at most 0.0045.
Values may be sent and summed in bfloat16 or wider, within the bound.
No kernel may reach another device: no remote copies, remote signals or barrier semaphores. Data moves between devices by JAX's collectives and lax.ppermute only.
A program may use at most 128 MiB of HBM per device.

v0:
```python
import math

import jax
import jax.numpy as jnp
from jax import lax
from jax.sharding import PartitionSpec as P

STEPS = 2


def shortened(x):

    def short(part):
        return part.astype(jnp.bfloat16) if part.dtype == jnp.float32 else part

    return jax.tree.map(short, x)


def shifted(x, axis, by):
    peers = lax.axis_size(axis)
    pairs = [(i, i + by) for i in range(peers) if 0 <= i + by < peers]
    return lax.ppermute(x, axis, pairs)


def kinetic_matrix(points):
    node_count = points + 1
    grid_index = jnp.arange(1, node_count, dtype=jnp.int32)
    row_index = grid_index[:, None]
    col_index = grid_index[None, :]
    distance = row_index - col_index
    summed = row_index + col_index
    nonzero_gap = jnp.where(distance == 0, 1, distance).astype(jnp.float32)
    inverse_gap = 1.0 / jnp.sin(math.pi * nonzero_gap / (2.0 * node_count)) ** 2
    inverse_sum = 1.0 / jnp.sin(math.pi * summed.astype(jnp.float32) / (2.0 * node_count)) ** 2
    parity = (1 - 2 * (jnp.abs(distance) % 2)).astype(jnp.float32)
    diagonal_values = (2.0 * node_count * node_count + 1.0) / 3.0 - 1.0 / jnp.sin(
        math.pi * grid_index.astype(jnp.float32) / node_count
    ) ** 2
    matrix = jnp.where(
        distance == 0, diagonal_values[:, None], parity * (inverse_gap - inverse_sum)
    )
    return matrix * (0.25 / (node_count * node_count))


def radial_profiles(points):
    radial_index = jnp.arange(points, dtype=jnp.int32).astype(jnp.float32)
    centrifugal = 0.1 / (1.0 + 8.0 * radial_index / points) ** 2
    beyond = jnp.maximum(radial_index - float(3 * points // 4), 0.0)
    damping = jnp.exp(-0.002 * beyond * beyond)
    return (centrifugal, damping)


def body(psi_prev, psi_cur, blocks, radial_terms, energies, rotation, coriolis, counts, offsets):
    hel_dev, chan_width, points = psi_cur.shape
    block_count = lax.axis_size("chan")
    block_index = lax.axis_index("chan")
    chan_ids = block_index * chan_width + jnp.arange(chan_width, dtype=jnp.int32)
    active = (chan_ids[None, :] < counts[:, None]).astype(jnp.float32)[:, :, None]
    local_blocks = blocks[:, 0]
    diagonal_block = local_blocks[:, 0]
    side_blocks = local_blocks[:, 1:]
    kinetic = kinetic_matrix(points)
    centrifugal, damping = radial_profiles(points)
    targets = (block_index + offsets) % block_count
    previous = active * psi_prev
    current = active * psi_cur
    for iteration in range(STEPS):
        psi_half = current.astype(jnp.bfloat16)
        weighted = (psi_half.astype(jnp.float32)[None] * radial_terms[:, None, None, :]).astype(
            jnp.bfloat16
        )
        shard_piece = lax.all_gather(psi_half, "chan", axis=1, tiled=True)
        piece_count = shard_piece.shape[1] // chan_width
        pieces = shard_piece.reshape(hel_dev, piece_count, chan_width, points)
        chosen_mask = (
            targets[:, :, None] == jnp.arange(piece_count, dtype=jnp.int32)[None, None, :]
        ).astype(jnp.bfloat16)
        chosen = jnp.einsum(
            "hjp,hpcr->hjcr", chosen_mask, pieces, preferred_element_type=jnp.float32
        )
        remote = chosen.astype(jnp.bfloat16)
        remote_weighted = (
            remote.astype(jnp.float32)[None] * radial_terms[:, None, None, None, :]
        ).astype(jnp.bfloat16)
        forward = jnp.einsum(
            "hjlcd,lhjdr->hcr", side_blocks, remote_weighted, preferred_element_type=jnp.float32
        )
        diagonal_term = jnp.einsum(
            "hlcd,lhdr->hcr", diagonal_block, weighted, preferred_element_type=jnp.float32
        )
        diagonal_term = diagonal_term + jnp.einsum(
            "hldc,lhdr->hcr", diagonal_block, weighted, preferred_element_type=jnp.float32
        )
        products = jnp.einsum(
            "hjlcd,lhcr->hjdr", side_blocks, weighted, preferred_element_type=jnp.float32
        )
        row_ids = jnp.arange(1 * lax.axis_size("chan"), dtype=jnp.int32)
        slot_mask = (targets[None, :, :] == row_ids[:, None, None]).astype(jnp.float32)
        returned = lax.psum_scatter(
            jnp.einsum(
                "qhj,hjdr->qhdr", slot_mask, products, precision=lax.Precision.HIGHEST
            ).astype(jnp.bfloat16),
            "chan",
            scatter_dimension=0,
            tiled=True,
        ).astype(jnp.float32)[0]
        coupling = diagonal_term + forward + returned
        kinetic_term = jnp.dot(
            current.reshape(-1, points),
            kinetic,
            precision=lax.Precision.HIGHEST,
            preferred_element_type=jnp.float32,
        ).reshape(current.shape)
        from_lower = shifted(shortened(coriolis[-1][:, None] * current[-1]), "hel", 1)
        from_upper = shifted(shortened(current[0]), "hel", -1)
        above_field = jnp.concatenate([current[1:], from_upper[None]], axis=0)
        below_term = jnp.concatenate(
            [from_lower[None], coriolis[:-1, :, None] * current[:-1]], axis=0
        )
        summed = (
            kinetic_term
            + (energies[:, :, None] + centrifugal * rotation[:, :, None]) * current
            + coupling
        )
        summed = summed - centrifugal * (coriolis[:, :, None] * above_field + below_term)
        renewed = damping * (2.0 * (active * summed) - damping * previous)
        previous = current
        current = renewed
    return (previous, current)


def solution(mesh):
    in_specs = (
        P("hel", "chan", None),
        P("hel", "chan", None),
        P("hel", "chan", None, None, None, None),
        P(),
        P("hel", "chan"),
        P("hel", "chan"),
        P("hel", "chan"),
        P("hel"),
        P("hel", None),
    )
    out_specs = (P("hel", "chan", None), P("hel", "chan", None))
    return jax.shard_map(body, mesh=mesh, in_specs=in_specs, out_specs=out_specs, check_vma=False)
```

profile of v0, /device:TPU:0, one launch (start us, length us, event | category | flops | bytes accessed | tf_op | source)
XLA Modules:
  0.0 686.4 jit_solution(12485358423854336883)
XLA Ops:
  7.2 0.7 compare_convert_fusion
  8.0 1.8 fusion.139
  9.8 1.1 copy.11
  10.9 4.3 copy.75
  15.2 2.7 copy-done
  17.9 3.5 fusion.10
  21.4 2.5 copy.33
  23.9 5.5 fusion.16
  29.5 6.3 copy.73
  35.8 0.6 copy-done.20
  36.5 1.3 collective-permute-start.1
  37.8 0.8 slice_bitcast_fusion.8
  38.7 1.5 collective-permute-start
  40.2 0.6 divide_subtract_fusion
  40.8 0.6 fusion.124
  41.4 2.7 fusion.46
  44.1 0.9 slice_multiply_fusion.1
  45.0 0.5 iota_add_fusion
  45.6 0.7 bitcast_convert_fusion.3
  46.2 61.4 %all-gather.3.cloned.1.call-done = bf16[3,4096,256]{2,1,0:T(8,128)(2,1)} async-done(((bf16[3,128,256]{2,1,0:T(8,128)(2,1)}), bf16[3,4096,256]{2,1,0:T(8,128)(2,1)}) %all-gather.3.cloned.1.call-update) | async-done | bytes 6291472 | tf_op jit(solution)/shard_map/all_gather | solution.py:72
  107.6 6.3 fusion.8
  113.9 1.2 copy.28
  115.1 0.3 convert_element_type.263
  115.5 6.7 fusion.38
  122.3 220.0 %reduce-scatter.3.cloned.1.call-done = bf16[1,3,128,256]{3,2,1,0:T(8,128)(2,1)} async-done(((bf16[32,3,128,256]{3,2,1,0:T(8,128)(2,1)}), bf16[1,3,128,256]{3,2,1,0:T(8,128)(2,1)}) %reduce-scatter.3.cloned.1.call-update) | async-done | bytes 196624 | tf_op jit(solution)/shard_map/reduce_scatter | solution.py:99
  342.3 2.1 fusion.63
  344.5 3.4 fusion.140
  348.3 1.1 copy.18
  349.3 0.7 copy-done.6
  350.1 6.0 fusion.12
  356.0 2.6 copy.43
  358.6 5.5 fusion.14
  364.2 6.3 copy.74
  370.5 1.0 copy-done.1
  371.5 1.3 collective-permute-start.3
  372.8 0.8 slice_bitcast_fusion.7
  373.7 0.8 slice_multiply_fusion
  374.5 2.8 fusion.44
  377.3 1.5 collective-permute-start.2
  378.8 2.5 collective-permute-done.2
  381.4 0.7 bitcast_convert_fusion.1
  382.0 57.2 %all-gather.5.cloned.1.call-done = bf16[3,4096,256]{2,1,0:T(8,128)(2,1)} async-done(((bf16[3,128,256]{2,1,0:T(8,128)(2,1)}), bf16[3,4096,256]{2,1,0:T(8,128)(2,1)}) %all-gather.5.cloned.1.call-update) | async-done | bytes 6291472 | tf_op jit(solution)/shard_map/all_gather | solution.py:72
  439.2 6.3 fusion.6
  445.5 1.2 copy.38
  447.2 6.7 fusion.41
  453.9 219.9 %reduce-scatter.5.cloned.1.call-done = bf16[1,3,128,256]{3,2,1,0:T(8,128)(2,1)} async-done(((bf16[32,3,128,256]{3,2,1,0:T(8,128)(2,1)}), bf16[1,3,128,256]{3,2,1,0:T(8,128)(2,1)}) %reduce-scatter.5.cloned.1.call-update) | async-done | bytes 196624 | tf_op jit(solution)/shard_map/reduce_scatter | solution.py:99
  673.8 2.1 fusion.67
  676.0 3.4 fusion.59
  (94 shorter events, 1.1 us)
Async XLA Ops:
  7.2 100.5 %all-gather.3.cloned.1.call-start = ((), (), s32[]{:S(2)}) async-start(), calls=%async_computation.2 | async-start | bytes 6488064 | tf_op jit(solution)/shard_map/all_gather | solution.py:72
  9.8 332.5 %reduce-scatter.3.cloned.1.call-start = ((), (), s32[]{:S(2)}) async-start(), calls=%async_computation.3 | async-start | bytes 6488064 | tf_op jit(solution)/shard_map/reduce_scatter | solution.py:99
  10.9 4.3 copy-start.3
  10.9 7.0 %copy-start.24 = (f32[8,256]{1,0:T(8,128)S(1)}, f32[8,256]{1,0:T(8,128)}, u32[]{:S(2)}) copy-start(f32[8,256]{1,0:T(8,128)} %param.12) | copy-start | bytes 24580
  15.2 2.7 copy-start
  21.4 2.6 copy-start.15
  35.8 0.7 copy-start.20
  35.8 5.6 copy-start.4
  35.8 5.6 copy-start.25
  35.8 403.4 %all-gather.5.cloned.1.call-start = ((), (), s32[]{:S(2)}) async-start(), calls=%async_computation.4 | async-start | bytes 6488064 | tf_op jit(solution)/shard_map/all_gather | solution.py:72
  36.5 9.0 %collective-permute-start.1 = (bf16[128,256]{1,0:T(8,128)(2,1)S(1)}, bf16[128,256]{1,0:T(8,128)(2,1)S(1)}, u32[]{:S(2)}, u32[]{:S(2)}) collective-permute-start(bf16[128,256]{1,0:T(8,128)(2,1)S(1)} %fusion.94), channel_id=1, source_target_pairs={{0,1},{1,2},{2,3},{4,5},{5,6},{6,7},{8,9},{9,10},{10,11},{12,13},{... | collective-permute-start | bytes 196616 | tf_op jit(solution)/shard_map/ppermute | solution.py:22
  38.7 6.9 %collective-permute-start = (bf16[128,256]{1,0:T(8,128)(2,1)S(1)}, bf16[128,256]{1,0:T(8,128)(2,1)S(1)}, u32[]{:S(2)}, u32[]{:S(2)}) collective-permute-start(bf16[128,256]{1,0:T(8,128)(2,1)S(1)} %slice_bitcast_fusion.8), channel_id=1, source_target_pairs={{1,0},{2,1},{3,2},{5,4},{6,5},{7,6},{9,8},{10,9},{11,10},{13,12},{... | collective-permute-start | bytes 196616 | tf_op jit(solution)/shard_map/ppermute | solution.py:22
  113.9 1.5 copy-start.26
  115.4 226.9 %copy-start.5 = (f32[3,128,256]{1,2,0:T(8,128)S(1)}, f32[3,128,256]{1,2,0:T(8,128)}, u32[]{:S(2)}) copy-start(f32[3,128,256]{1,2,0:T(8,128)} %copy-done.3) | copy-start | bytes 1179652
  115.4 226.9 %copy-start.38 = (f32[3,256,128]{1,2,0:T(8,128)S(1)}, f32[3,256,128]{1,2,0:T(8,128)}, u32[]{:S(2)}) copy-start(f32[3,256,128]{1,2,0:T(8,128)} %fusion.46) | copy-start | bytes 1179652
  115.4 229.0 %copy-start.11 = (f32[2,128,256]{2,1,0:T(8,128)S(1)}, f32[2,128,256]{2,1,0:T(8,128)}, u32[]{:S(2)}) copy-start(f32[2,128,256]{2,1,0:T(8,128)} %get-tuple-element.6) | copy-start | bytes 786436
  115.4 229.0 %copy-start.12 = (f32[2,128,256]{2,1,0:T(8,128)S(1)}, f32[2,128,256]{2,1,0:T(8,128)}, u32[]{:S(2)}) copy-start(f32[2,128,256]{2,1,0:T(8,128)} %get-tuple-element.7) | copy-start | bytes 786436
  115.4 229.0 %copy-start.14 = (f32[1,128,256]{2,1,0:T(8,128)S(1)}, f32[1,128,256]{2,1,0:T(8,128)}, u32[]{:S(2)}) copy-start(f32[1,128,256]{2,1,0:T(8,128)} %bitcast_convert_fusion.3) | copy-start | bytes 393220
  115.5 229.0 %copy-start.16 = (f32[256]{0:T(256)S(1)}, f32[256]{0:T(256)}, u32[]{:S(2)}) copy-start(f32[256]{0:T(256)} %get-tuple-element.10) | copy-start | bytes 3076
  115.5 229.0 %copy-start.18 = (f32[256]{0:T(256)S(1)}, f32[256]{0:T(256)}, u32[]{:S(2)}) copy-start(f32[256]{0:T(256)} %get-tuple-element.11) | copy-start | bytes 3076
  115.5 229.0 %copy-start.21 = (f32[3,128]{1,0:T(4,128)S(1)}, f32[3,128]{1,0:T(4,128)}, u32[]{:S(2)}) copy-start(f32[3,128]{1,0:T(4,128)} %param.15) | copy-start | bytes 4612
  115.5 229.0 %copy-start.23 = (f32[3,128,256]{2,1,0:T(8,128)S(1)}, f32[3,128,256]{2,1,0:T(8,128)}, u32[]{:S(2)}) copy-start(f32[3,128,256]{2,1,0:T(8,128)} %param.9) | copy-start | bytes 1179652
  115.5 229.0 %copy-start.29 = (f32[3,128]{1,0:T(4,128)S(1)}, f32[3,128]{1,0:T(4,128)}, u32[]{:S(2)}) copy-start(f32[3,128]{1,0:T(4,128)} %param.14) | copy-start | bytes 4612
  115.5 229.0 %copy-start.31 = (f32[3,128]{1,0:T(4,128)S(1)}, f32[3,128]{1,0:T(4,128)}, u32[]{:S(2)}) copy-start(f32[3,128]{1,0:T(4,128)} %param.13) | copy-start | bytes 4612
  115.5 229.0 %copy-start.33 = (f32[256]{0:T(256)S(1)}, f32[256]{0:T(256)}, u32[]{:S(2)}) copy-start(f32[256]{0:T(256)} %divide_subtract_fusion) | copy-start | bytes 3076
  115.5 229.0 %copy-start.35 = (s32[256]{0:T(256)S(1)}, s32[256]{0:T(256)}, u32[]{:S(2)}) copy-start(s32[256]{0:T(256)} %iota_add_fusion) | copy-start | bytes 3076
  348.0 325.8 %reduce-scatter.5.cloned.1.call-start = ((), (), s32[]{:S(2)}) async-start(), calls=%async_computation.5 | async-start | bytes 6488064 | tf_op jit(solution)/shard_map/reduce_scatter | solution.py:99
  349.3 0.7 copy-start.6
  370.4 1.0 copy-start.1
  370.4 4.1 copy-start.7
  370.4 4.1 copy-start.27
  371.5 7.3 %collective-permute-start.3 = (bf16[128,256]{1,0:T(8,128)(2,1)S(1)}, bf16[128,256]{1,0:T(8,128)(2,1)S(1)}, u32[]{:S(2)}, u32[]{:S(2)}) collective-permute-start(bf16[128,256]{1,0:T(8,128)(2,1)S(1)} %fusion.92), channel_id=1, source_target_pairs={{0,1},{1,2},{2,3},{4,5},{5,6},{6,7},{8,9},{9,10},{10,11},{12,13},{... | collective-permute-start | bytes 196616 | tf_op jit(solution)/shard_map/ppermute | solution.py:22
  377.3 4.1 collective-permute-start.2
  445.5 1.5 copy-start.28
  447.0 226.8 %copy-start.8 = (f32[3,128,256]{1,2,0:T(8,128)S(1)}, f32[3,128,256]{1,2,0:T(8,128)}, u32[]{:S(2)}) copy-start(f32[3,128,256]{1,2,0:T(8,128)} %copy-done.6) | copy-start | bytes 1179652
  447.0 226.8 %copy-start.37 = (f32[3,256,128]{1,2,0:T(8,128)S(1)}, f32[3,256,128]{1,2,0:T(8,128)}, u32[]{:S(2)}) copy-start(f32[3,256,128]{1,2,0:T(8,128)} %fusion.44) | copy-start | bytes 1179652
  447.0 228.9 %copy-start.2 = (f32[3,128,256]{2,1,0:T(8,128)S(1)}, f32[3,128,256]{2,1,0:T(8,128)}, u32[]{:S(2)}) copy-start(f32[3,128,256]{2,1,0:T(8,128)} %get-tuple-element.9) | copy-start | bytes 1179652
  447.0 228.9 %copy-start.9 = (f32[2,128,256]{2,1,0:T(8,128)S(1)}, f32[2,128,256]{2,1,0:T(8,128)}, u32[]{:S(2)}) copy-start(f32[2,128,256]{2,1,0:T(8,128)} %get-tuple-element.4) | copy-start | bytes 786436
  447.1 228.9 %copy-start.10 = (f32[2,128,256]{2,1,0:T(8,128)S(1)}, f32[2,128,256]{2,1,0:T(8,128)}, u32[]{:S(2)}) copy-start(f32[2,128,256]{2,1,0:T(8,128)} %get-tuple-element.5) | copy-start | bytes 786436
  447.1 228.9 %copy-start.13 = (f32[1,128,256]{2,1,0:T(8,128)S(1)}, f32[1,128,256]{2,1,0:T(8,128)}, u32[]{:S(2)}) copy-start(f32[1,128,256]{2,1,0:T(8,128)} %bitcast_convert_fusion.1) | copy-start | bytes 393220
  447.1 228.9 %copy-start.17 = (f32[256]{0:T(256)S(1)}, f32[256]{0:T(256)}, u32[]{:S(2)}) copy-start(f32[256]{0:T(256)} %get-tuple-element.10) | copy-start | bytes 3076
  447.1 228.9 %copy-start.19 = (f32[256]{0:T(256)S(1)}, f32[256]{0:T(256)}, u32[]{:S(2)}) copy-start(f32[256]{0:T(256)} %get-tuple-element.11) | copy-start | bytes 3076
  447.1 228.9 %copy-start.22 = (f32[3,128]{1,0:T(4,128)S(1)}, f32[3,128]{1,0:T(4,128)}, u32[]{:S(2)}) copy-start(f32[3,128]{1,0:T(4,128)} %param.15) | copy-start | bytes 4612
  447.1 228.9 %copy-start.30 = (f32[3,128]{1,0:T(4,128)S(1)}, f32[3,128]{1,0:T(4,128)}, u32[]{:S(2)}) copy-start(f32[3,128]{1,0:T(4,128)} %param.14) | copy-start | bytes 4612
  447.1 228.9 %copy-start.32 = (f32[3,128]{1,0:T(4,128)S(1)}, f32[3,128]{1,0:T(4,128)}, u32[]{:S(2)}) copy-start(f32[3,128]{1,0:T(4,128)} %param.13) | copy-start | bytes 4612
  447.1 228.9 %copy-start.34 = (f32[256]{0:T(256)S(1)}, f32[256]{0:T(256)}, u32[]{:S(2)}) copy-start(f32[256]{0:T(256)} %divide_subtract_fusion) | copy-start | bytes 3076
  447.1 228.9 %copy-start.36 = (s32[256]{0:T(256)S(1)}, s32[256]{0:T(256)}, u32[]{:S(2)}) copy-start(s32[256]{0:T(256)} %iota_add_fusion) | copy-start | bytes 3076
Sparse Core Ops, SparseCore 0:
  11.1 96.4 all-gather.2
  112.8 229.5 reduce-scatter.2
  348.1 91.0 all-gather.4
  444.2 229.5 reduce-scatter.4
where the time goes:
time: 695 us; the launch traced here: 686 us
  waiting for transfers between devices  561 us (81%)
  matrix products  63 us (9%)
  local copies, waits for them, and re-layouts  33.3 us (5%)
  between operations  14.9 us (2%)
  other arithmetic  8.11 us (1%)
    reduce_scatter x2, waiting for transfers between devices, body(): lax.psum_scatter(jnp.einsum('qhj,hjdr->qhdr', slot_mask, products, precis...  440 us
    all_gather x2, waiting for transfers between devices, body(): shard_piece = lax.all_gather(psi_half, 'chan', axis=1, tiled=True)  119 us
  transfers between devices with their start and end apart: 8, of which 5 were waited for; matrix products, arithmetic and copies ran while one was open for 12% of the time, Pallas kernels for 0%

commit v1 on v0

v1 whole, which is shorter than its diff:
```python
import functools

import jax
import jax.numpy as jnp
import numpy as np
from jax import lax
from jax.experimental import pallas as pl
from jax.experimental.pallas import tpu as pltpu
from jax.sharding import PartitionSpec as P

STEPS = 2
BF = jnp.bfloat16
F32 = jnp.float32
VMEM_LIMIT = 40 * 1024 * 1024
ROUTED = (0, 1, 2, 3, 4, 5, 6)


def kinetic_matrix(points):
    n = points + 1
    i = np.arange(1, n, dtype=np.float64)[:, None]
    k = i.T
    gap = np.where(i == k, 1.0, i - k)
    parity = 1.0 - 2.0 * (np.abs(i - k) % 2)
    off = parity * (1.0 / np.sin(np.pi * gap / (2 * n)) ** 2 - 1.0 / np.sin(np.pi * (i + k) / (2 * n)) ** 2)
    diagonal = (2.0 * n * n + 1.0) / 3.0 - 1.0 / np.sin(np.pi * i / n) ** 2
    return (np.where(i == k, diagonal, off) * (0.25 / (n * n))).astype(np.float32)


def radial_profiles(points, width):
    r = np.arange(points, dtype=np.float64)
    centrifugal = 0.1 / (1.0 + 8.0 * r / points) ** 2
    damping = np.exp(-0.002 * np.maximum(r - 3 * points // 4, 0.0) ** 2)
    spread = lambda v: np.ascontiguousarray(np.broadcast_to(v.astype(np.float32)[:, None], (points, width)))
    return spread(centrifugal), spread(damping)


def dot_nn(a, b):
    return lax.dot_general(a, b, (((1,), (0,)), ((), ())), preferred_element_type=F32)


def dot_nt(a, b):
    return lax.dot_general(a, b, (((1,), (1,)), ((), ())), preferred_element_type=F32)


def active_row(remaining_ref, h, width):
    lane = lax.broadcasted_iota(jnp.int32, (1, width), 1)
    return (lane < remaining_ref[h]).astype(F32)


def radial_column(rt_ref, term, shape):
    return jnp.broadcast_to(rt_ref[:, term : term + 1], shape)


def emit_products(h, field, blocks_ref, rt_ref, pieces_ref):
    points, width = field.shape
    terms = blocks_ref.shape[3]
    half = field.astype(BF)
    wide = half.astype(F32)
    weighted = jnp.concatenate(
        [(wide * radial_column(rt_ref, l, field.shape)).astype(BF) for l in range(terms)], axis=1
    )
    per = 1 + len(ROUTED)
    slots = pieces_ref.shape[1:]
    pieces_ref[h * per] = wide.reshape(slots)
    for start in range(0, len(ROUTED), 2):
        pair = ROUTED[start : start + 2]
        rhs = jnp.concatenate([blocks_ref[0, 0, 1 + j].reshape(terms * width, width) for j in pair], axis=1)
        out = dot_nn(weighted, rhs)
        for k in range(len(pair)):
            pieces_ref[h * per + 1 + start + k] = out[:, k * width : (k + 1) * width].reshape(slots)


def emit_pieces(pieces_ref, send_ref):
    count = pieces_ref.shape[0]
    rows, width = pieces_ref.shape[2:]

    def step(i, carry):
        for u in range(2):
            n = 2 * i + u
            send_ref[n] = pieces_ref[:, n].reshape(count * rows, width).astype(BF)
        return carry

    lax.fori_loop(0, send_ref.shape[0] // 2, step, 0)


def emit_edges(h, last, field, cor_ref, up_ref, down_ref):
    @pl.when(h == last)
    def _():
        up_ref[...] = (field * cor_ref[last : last + 1, :]).astype(BF)

    @pl.when(h == 0)
    def _():
        down_ref[...] = field.astype(BF)


def first_kernel(remaining_ref, psi_ref, blocks_ref, rt_ref, cor_ref, field_ref, send_ref, up_ref, down_ref, pieces_ref):
    h = pl.program_id(0)
    last = pl.num_programs(0) - 1
    field = psi_ref[0].T * active_row(remaining_ref, h, psi_ref.shape[1])
    field_ref[0] = field
    emit_edges(h, cor_ref.shape[0] - 1, field, cor_ref, up_ref, down_ref)
    emit_products(h, field, blocks_ref, rt_ref, pieces_ref)

    @pl.when(h == last)
    def _():
        emit_pieces(pieces_ref, send_ref)


def route_kernel(offsets_ref, got_ref, send_ref, wide_ref):
    count, rows, width = got_ref.shape
    helicities = offsets_ref.shape[0]
    per = 1 + len(ROUTED)
    piece = rows // (helicities * per)

    def widen(b, carry):
        for u in range(2):
            wide_ref[2 * b + u] = got_ref[2 * b + u].astype(F32)
        return carry

    lax.fori_loop(0, count // 2, widen, 0)

    def step(d, carry):
        out = []
        for h in range(helicities):
            base = h * per * piece
            total = None
            for k, j in enumerate(ROUTED):
                turn = offsets_ref[h, j]
                ahead = (d + turn) & (count - 1)
                behind = (d - turn) & (count - 1)
                out.append(wide_ref[ahead, base : base + piece, :])
                at = base + (1 + k) * piece
                term = wide_ref[behind, at : at + piece, :]
                total = term if total is None else total + term
            out.append(total)
        send_ref[d] = jnp.concatenate(out, axis=0).astype(BF)
        return carry

    lax.fori_loop(0, count, step, 0)


def local_kernel(
    transposed, remaining_ref, field_ref, prev_ref, diag_ref, rt_ref, kin_ref, cent_ref, damp_ref, e_ref, rot_ref, cor_ref, out_ref
):
    helicities, points, width = field_ref.shape
    terms = diag_ref.shape[3 - 1]
    cent = cent_ref[...]
    damp = damp_ref[...]
    for h in range(helicities):
        mask = active_row(remaining_ref, h, width)
        field = field_ref[h]
        half = field.astype(BF)
        total = lax.dot_general(
            kin_ref[...], field, (((1,), (0,)), ((), ())), precision=lax.Precision.HIGHEST, preferred_element_type=F32
        )
        for l in range(terms):
            block = diag_ref[h, 0, l]
            total = total + radial_column(rt_ref, l, field.shape) * (dot_nn(half, block) + dot_nt(half, block))
        total = total + (e_ref[h : h + 1, :] + cent * rot_ref[h : h + 1, :]) * field
        if h + 1 < helicities:
            total = total - cent * (cor_ref[h : h + 1, :] * field_ref[h + 1])
        if h > 0:
            total = total - cent * (cor_ref[h - 1 : h, :] * field_ref[h - 1])
        previous = prev_ref[h] if transposed else prev_ref[h].T * mask
        out_ref[h] = damp * (2.0 * (mask * total) - damp * previous)


def renew(h, remaining_ref, local_ref, sources_ref, blocks_ref, rt_ref, cent_ref, damp_ref, cor_ref, below_ref, above_ref):
    _, points, width = local_ref.shape
    terms = blocks_ref.shape[3]
    helicities = cor_ref.shape[0]
    per = 1 + len(ROUTED)
    shape = (points, width)
    sources = jnp.concatenate(
        [sources_ref[h * per + k].reshape(shape).astype(BF) for k in range(len(ROUTED))], axis=1
    )
    total = sources_ref[h * per + len(ROUTED)].reshape(shape)
    for l in range(0, terms, 2):
        rhs = jnp.concatenate(
            [jnp.concatenate([blocks_ref[0, 0, 1 + j, l + u] for j in ROUTED], axis=1) for u in range(2)], axis=0
        )
        out = dot_nt(sources, rhs)
        for u in range(2):
            total = total + radial_column(rt_ref, l + u, shape) * out[:, u * width : (u + 1) * width]
    below = jnp.where(h == 0, 1.0, 0.0) * below_ref[...].astype(F32)
    above = jnp.where(h == helicities - 1, 1.0, 0.0) * above_ref[...].astype(F32) * cor_ref[helicities - 1 : helicities, :]
    total = total - cent_ref[...] * (below + above)
    return local_ref[0] + 2.0 * damp_ref[...] * (active_row(remaining_ref, h, width) * total)


def unpack(got_ref, sources_ref):
    count, rows, width = got_ref.shape
    slots, _, piece, _ = sources_ref.shape

    def step(i, carry):
        for u in range(2):
            n = 2 * i + u
            sources_ref[:, n] = got_ref[n].astype(F32).reshape(slots, piece, width)
        return carry

    lax.fori_loop(0, count // 2, step, 0)


def middle_kernel(
    remaining_ref, got_ref, local_ref, blocks_ref, rt_ref, cent_ref, damp_ref, cor_ref, below_ref, above_ref,
    field_ref, send_ref, up_ref, down_ref, sources_ref, pieces_ref,
):
    h = pl.program_id(0)

    @pl.when(h == 0)
    def _():
        unpack(got_ref, sources_ref)

    field = renew(
        h, remaining_ref, local_ref, sources_ref, blocks_ref, rt_ref, cent_ref, damp_ref, cor_ref, below_ref, above_ref
    )
    field_ref[0] = field
    emit_edges(h, cor_ref.shape[0] - 1, field, cor_ref, up_ref, down_ref)
    emit_products(h, field, blocks_ref, rt_ref, pieces_ref)

    @pl.when(h == pl.num_programs(0) - 1)
    def _():
        emit_pieces(pieces_ref, send_ref)


def last_kernel(
    remaining_ref, got_ref, local_ref, blocks_ref, rt_ref, cent_ref, damp_ref, cor_ref, below_ref, above_ref, field_ref,
    before_ref, last_ref, sources_ref,
):
    h = pl.program_id(0)

    @pl.when(h == 0)
    def _():
        unpack(got_ref, sources_ref)

    field = renew(
        h, remaining_ref, local_ref, sources_ref, blocks_ref, rt_ref, cent_ref, damp_ref, cor_ref, below_ref, above_ref
    )
    last_ref[0] = field.T
    before_ref[0] = field_ref[0].T


def shifted(x, axis, by):
    peers = lax.axis_size(axis)
    return lax.ppermute(x, axis, [(i, i + by) for i in range(peers) if 0 <= i + by < peers])


def exchange(x):
    return lax.all_to_all(x, "chan", 0, 0, tiled=True)


def body(psi_prev, psi_cur, blocks, radial_terms, energies, rotation, coriolis, counts, offsets):
    helicities, width, points = psi_cur.shape
    count = lax.axis_size("chan")
    terms = blocks.shape[3]
    piece = points // count
    per = 1 + len(ROUTED)
    rows = helicities * per * piece
    remaining = counts - lax.axis_index("chan").astype(jnp.int32) * width
    rt = radial_terms.T
    kinetic = jnp.asarray(kinetic_matrix(points))
    cent, damp = (jnp.asarray(v) for v in radial_profiles(points, width))

    smem = pl.BlockSpec(memory_space=pltpu.SMEM)
    whole = lambda a: pl.BlockSpec(a, lambda *_: (0,) * len(a))
    by_h = lambda a: pl.BlockSpec((1,) + a[1:], lambda h: (h,) + (0,) * (len(a) - 1))
    sds = jax.ShapeDtypeStruct
    params = lambda: pltpu.CompilerParams(vmem_limit_bytes=VMEM_LIMIT)
    cost = lambda flops, moved: pl.CostEstimate(flops=flops, bytes_accessed=moved, transcendentals=0)

    field_shape = (helicities, points, width)
    field_out = sds(field_shape, F32)
    parcel = sds((count, rows, width), BF)
    edge = sds((points, width), BF)
    parts = pltpu.VMEM((helicities * per, count, piece, width), F32)
    mac = 2 * helicities * points * width * width * terms
    side = blocks.shape[2] - 1

    first = pl.pallas_call(
        first_kernel,
        grid=(helicities,),
        in_specs=[smem, by_h(psi_cur.shape), by_h(blocks.shape), whole(rt.shape), whole(coriolis.shape)],
        out_specs=[by_h(field_shape), whole(parcel.shape), whole(edge.shape), whole(edge.shape)],
        out_shape=[field_out, parcel, edge, edge],
        scratch_shapes=[parts],
        compiler_params=params(),
        cost_estimate=cost(side * mac, blocks.size * 2),
    )
    route = pl.pallas_call(
        route_kernel,
        in_specs=[smem, whole(parcel.shape)],
        out_specs=whole(parcel.shape),
        out_shape=parcel,
        grid=(1,),
        scratch_shapes=[pltpu.VMEM(parcel.shape, F32)],
        compiler_params=params(),
        cost_estimate=cost(parcel.size * 4, parcel.size * 4),
    )

    def local(transposed, prev):
        diag = (helicities, 1, 1) + blocks.shape[3:]

        def kernel(remaining_ref, field_ref, prev_ref, diag_ref, *rest):
            local_kernel(transposed, remaining_ref, field_ref, prev_ref, diag_ref.at[:, 0], *rest)

        return pl.pallas_call(
            kernel,
            grid=(1,),
            in_specs=[
                smem, whole(field_shape), whole(prev.shape), whole(diag), whole(rt.shape), whole(kinetic.shape), whole(cent.shape),
                whole(damp.shape), whole(energies.shape), whole(rotation.shape), whole(coriolis.shape),
            ],
            out_specs=whole(field_shape),
            out_shape=field_out,
            compiler_params=params(),
            cost_estimate=cost(2 * mac, 4 * psi_cur.size),
        )

    renew_specs = [
        smem, whole(parcel.shape), by_h(field_shape), by_h(blocks.shape), whole(rt.shape), whole(cent.shape), whole(damp.shape),
        whole(coriolis.shape), whole(edge.shape), whole(edge.shape),
    ]
    middle = pl.pallas_call(
        middle_kernel,
        grid=(helicities,),
        in_specs=renew_specs,
        out_specs=[by_h(field_shape), whole(parcel.shape), whole(edge.shape), whole(edge.shape)],
        out_shape=[field_out, parcel, edge, edge],
        scratch_shapes=[parts, parts],
        compiler_params=params(),
        cost_estimate=cost(2 * side * mac, blocks.size * 2),
    )
    final = pl.pallas_call(
        last_kernel,
        grid=(helicities,),
        in_specs=renew_specs + [by_h(field_shape)],
        out_specs=[by_h(psi_cur.shape), by_h(psi_cur.shape)],
        out_shape=[sds(psi_cur.shape, F32)] * 2,
        scratch_shapes=[parts],
        compiler_params=params(),
        cost_estimate=cost(side * mac, blocks.size * 2),
    )

    field, send, up, down = first(remaining, psi_cur, blocks, rt, coriolis)
    prev = psi_prev
    for iteration in range(STEPS):
        below = shifted(up, "hel", 1)
        above = shifted(down, "hel", -1)
        got = exchange(send)
        rest = local(iteration > 0, prev)(
            remaining, field, prev, blocks, rt, kinetic, cent, damp, energies, rotation, coriolis
        )
        back = exchange(route(offsets, got))
        given = (remaining, back, rest, blocks, rt, cent, damp, coriolis, below, above)
        prev = field
        if iteration + 1 < STEPS:
            field, send, up, down = middle(*given)
        else:
            return tuple(final(*given, field))


def solution(mesh):
    in_specs = (
        P("hel", "chan", None),
        P("hel", "chan", None),
        P("hel", "chan", None, None, None, None),
        P(),
        P("hel", "chan"),
        P("hel", "chan"),
        P("hel", "chan"),
        P("hel"),
        P("hel", None),
    )
    out_specs = (P("hel", "chan", None), P("hel", "chan", None))
    return jax.shard_map(body, mesh=mesh, in_specs=in_specs, out_specs=out_specs, check_vma=False)
```

time: 695 us -> 158 us (0.23); the launches traced: 686 us -> 157 us
  waiting for transfers between devices: 561 us -> 29.7 us
  blocking collectives: 0 us -> 63.4 us
  matrix products: 63 us -> 0 us
  Pallas kernels: 0 us -> 27.7 us
  between operations: 14.9 us -> 0.86 us
  local copies, waits for them, and re-layouts: 33.3 us -> 19.4 us
  starting transfers between devices: 5.94 us -> 15.3 us
  other arithmetic: 8.11 us -> 0.66 us
    reduce_scatter x2 -> x0, waiting for transfers between devices: 440 us -> none  [body(): lax.psum_scatter(jnp.einsum('qhj,hjdr->qhdr', slot_mask, products, precis...]
    all_gather x2 -> x0, waiting for transfers between devices: 119 us -> none  [body(): shard_piece = lax.all_gather(psi_half, 'chan', axis=1, tiled=True)]
    all_to_all x0 -> x2, blocking collectives: none -> 63.4 us  [exchange(): return lax.all_to_all(x, 'chan', 0, 0, tiled=True)]
    dot_general x14 -> x0, matrix products: 63 us -> none  [the longest x2 13.5 us: body(): jnp.einsum('hjlcd,lhjdr->hcr', side_blocks, remote_weighted, preferred_el...]
    all_to_all x0 -> x2, waiting for transfers between devices: none -> 29.7 us  [exchange(): return lax.all_to_all(x, 'chan', 0, 0, tiled=True)]
    pallas_call x0 -> x7, Pallas kernels: none -> 27.7 us  [the longest x2 7.6 us: body(): back = exchange(route(offsets, got))]
    dot_general x6 -> x0, local copies, waits for them, and re-layouts: 20 us -> none  [the longest x2 12.5 us: body(): jnp.einsum('qhj,hjdr->qhdr', slot_mask, products, precision=lax.Precision...]
    unnamed x79 -> x41, local copies, waits for them, and re-layouts: 9.44 us -> 19.4 us
  transfers between devices with their start and end apart: 8 -> 6, of which waited for: 5 -> 2; matrix products, arithmetic and copies ran while one was open for 12% -> 0% of each run, Pallas kernels for 0% -> 3%
where the time goes in v1:
time: 158 us; the launch traced here: 157 us
  blocking collectives  63.4 us (40%)
  waiting for transfers between devices  29.7 us (19%)
  Pallas kernels  27.7 us (18%)
  local copies, waits for them, and re-layouts  19.4 us (12%)
  starting transfers between devices  15.3 us (10%)
    all_to_all x2, blocking collectives, exchange(): return lax.all_to_all(x, 'chan', 0, 0, tiled=True)  63.4 us
    all_to_all x2, waiting for transfers between devices, exchange(): return lax.all_to_all(x, 'chan', 0, 0, tiled=True)  29.7 us
    unnamed x41, local copies, waits for them, and re-layouts  19.4 us
    all_to_all x2, starting transfers between devices, exchange(): return lax.all_to_all(x, 'chan', 0, 0, tiled=True)  9.43 us
    pallas_call x2, Pallas kernels, body(): back = exchange(route(offsets, got))  7.6 us
    pallas_call x1, Pallas kernels, body(): field, send, up, down = middle(*given)  6.84 us
    ppermute x4, starting transfers between devices, shifted(): lax.ppermute(x, axis, [(i, i + by) for i in range(peers) if 0 <= i + by <...  5.86 us
    pallas_call x2, Pallas kernels, body(): local(iteration > 0, prev)  4.5 us
  transfers between devices with their start and end apart: 6, of which 2 were waited for; matrix products, arithmetic and copies ran while one was open for 0% of the time, Pallas kernels for 3%

profile of v1, /device:TPU:0, one launch (start us, length us, event | category | flops | bytes accessed | tf_op | source)
XLA Modules:
  0.0 157.0 jit_solution(5896778112593152268)
XLA Ops:
  0.6 0.8 copy.14
  1.5 0.7 broadcast_subtract_fusion.remaining_ref
  2.1 2.8 %copy-done = bf16[3,1,8,8,128,128]{5,4,3,2,1,0:T(8,128)(2,1)S(1)} copy-done((bf16[3,1,8,8,128,128]{5,4,3,2,1,0:T(8,128)(2,1)S(1)}, bf16[3,1,8,8,128,128]{5,4,3,2,1,0:T(8,128)(2,1)}, u32[]{:S(2)}) %copy-start) | copy-done | bytes 6291480
  4.9 1.0 copy-done.9
  5.9 0.7 copy-done.10
  6.6 4.5 %shard_map.131 = (f32[3,256,128]{2,1,0:T(8,128)S(1)}, bf16[32,192,128]{2,1,0:T(8,128)(2,1)S(1)}, bf16[256,128]{1,0:T(8,128)(2,1)}, bf16[256,128]{1,0:T(8,128)(2,1)}) custom-call(s32[3]{0:T(128)S(1)} %broadcast_subtract_fusion.remaining_ref, f32[3,128,256]{2,1,0:T(8,128)S(1)} %copy-done.9, bf16[3,1,8,8,128,128]{5,4,3,2,1,0:T(8,128)(2,1)S(1)} %copy-done, ...), custom_call_target="tpu_custom_call" | custom-call | flops 1409286144 | bytes 6291456 | tf_op jit(solution)/shard_map/pallas_call | solution.py:344
  11.1 34.7 %all_to_all.20.got_ref = bf16[32,192,128]{2,1,0:T(8,128)(2,1)S(1)} all-to-all(bf16[32,192,128]{2,1,0:T(8,128)(2,1)S(1)} %get-tuple-element.10), channel_id=1, replica_groups=mesh['chan'=32,'hel'=4] {'chan'}, dimensions={0} | all-to-all | bytes 3145728 | tf_op jit(solution)/shard_map/all_to_all | solution.py:249
  45.7 0.0 copy-done.14
  45.7 3.8 %shard_map.132 = bf16[32,192,128]{2,1,0:T(8,128)(2,1)} custom-call(s32[3,7]{1,0:T(4,128)S(1)} %copy-done.14, bf16[32,192,128]{2,1,0:T(8,128)(2,1)S(1)} %all_to_all.20.got_ref), custom_call_target="tpu_custom_call" | custom-call | flops 3145728 | bytes 3145728 | tf_op jit(solution)/shard_map/pallas_call | solution.py:353
  49.5 0.0 copy-start.11
  49.6 0.0 copy-start.12
  49.6 0.0 copy-start.13
  49.6 4.6 %all-to-all-start.1 = ((bf16[32,192,128]{2,1,0:T(8,128)(2,1)}), bf16[32,192,128]{2,1,0:T(8,128)(2,1)S(1)}, u32[]{:S(2)}, u32[]{:S(2)}) async-start(bf16[32,192,128]{2,1,0:T(8,128)(2,1)} %shard_map.132), calls=%async_computation.1 | async-start | bytes 3145728 | tf_op jit(solution)/shard_map/all_to_all | solution.py:249
  54.2 1.3 collective-permute-start
  55.5 1.3 collective-permute-start.1
  56.8 0.0 copy-done.5
  56.8 0.0 copy-done.6
  56.8 0.0 copy-done.7
  56.8 0.0 copy-done.8
  56.8 0.0 copy-done.11
  56.8 0.0 copy-done.12
  56.8 0.0 copy-done.13
  56.8 0.0 copy-start.1
  56.8 2.8 %copy-done.1 = bf16[3,1,8,8,128,128]{5,4,3,2,1,0:T(8,128)(2,1)S(1)} copy-done((bf16[3,1,8,8,128,128]{5,4,3,2,1,0:T(8,128)(2,1)S(1)}, bf16[3,1,8,8,128,128]{5,4,3,2,1,0:T(8,128)(2,1)}, u32[]{:S(2)}) %copy-start.1) | copy-done | bytes 6291480
  59.6 2.2 %shard_map.133.local_ref = f32[3,256,128]{2,1,0:T(8,128)S(1)} custom-call(s32[3]{0:T(128)S(1)} %broadcast_subtract_fusion.remaining_ref, f32[3,256,128]{2,1,0:T(8,128)S(1)} %get-tuple-element.11.field_ref.prev_ref, f32[3,128,256]{2,1,0:T(8,128)S(1)} %copy-done.8, bf16[3,1,8,8,128,128]{5,4,3,2,1,0:T(8,128)(2,1)S(1)} %copy-done.1, f32[256,8]{1,0:T(8,128)S(1)} %bitcast.2, ...), custom_call_target="tpu_custom_call" | custom-call | flops 402653184 | bytes 393216 | tf_op jit(solution)/shard_map/pallas_call | solution.py:350
  61.9 0.0 collective-permute-done.below_ref
  61.9 0.0 copy-start.16
  61.9 0.6 copy-done.16
  62.5 0.0 collective-permute-done.1.above_ref
  62.5 0.6 copy-done.18
  63.2 13.7 %all-to-all-done.1.got_ref = bf16[32,192,128]{2,1,0:T(8,128)(2,1)S(1)} async-done(((bf16[32,192,128]{2,1,0:T(8,128)(2,1)}), bf16[32,192,128]{2,1,0:T(8,128)(2,1)S(1)}, u32[]{:S(2)}, u32[]{:S(2)}) %all-to-all-start.1) | async-done | bytes 1572896 | tf_op jit(solution)/shard_map/all_to_all | solution.py:249
  76.8 2.8 %copy-done.2 = bf16[3,1,8,8,128,128]{5,4,3,2,1,0:T(8,128)(2,1)S(1)} copy-done((bf16[3,1,8,8,128,128]{5,4,3,2,1,0:T(8,128)(2,1)S(1)}, bf16[3,1,8,8,128,128]{5,4,3,2,1,0:T(8,128)(2,1)}, u32[]{:S(2)}) %copy-start.2) | copy-done | bytes 6291480
  79.6 0.8 copy-done.17
  80.5 0.8 copy-done.19
  81.3 6.8 %shard_map.134 = (f32[3,256,128]{2,1,0:T(8,128)S(1)}, bf16[32,192,128]{2,1,0:T(8,128)(2,1)S(1)}, bf16[256,128]{1,0:T(8,128)(2,1)}, bf16[256,128]{1,0:T(8,128)(2,1)S(1)}) custom-call(s32[3]{0:T(128)S(1)} %broadcast_subtract_fusion.remaining_ref, bf16[32,192,128]{2,1,0:T(8,128)(2,1)S(1)} %all-to-all-done.1.got_ref, f32[3,256,128]{2,1,0:T(8,128)S(1)} %shard_map.133.local_ref, ...), custom_call_target="tpu_custom_call" | custom-call | flops 2818572288 | bytes 6291456 | tf_op jit(solution)/shard_map/pallas_call | solution.py:357
  88.2 28.8 %all_to_all.21.got_ref = bf16[32,192,128]{2,1,0:T(8,128)(2,1)S(1)} all-to-all(bf16[32,192,128]{2,1,0:T(8,128)(2,1)S(1)} %get-tuple-element.14), channel_id=1, replica_groups=mesh['chan'=32,'hel'=4] {'chan'}, dimensions={0} | all-to-all | bytes 3145728 | tf_op jit(solution)/shard_map/all_to_all | solution.py:249
  116.9 3.8 %shard_map.135 = bf16[32,192,128]{2,1,0:T(8,128)(2,1)} custom-call(s32[3,7]{1,0:T(4,128)S(1)} %copy-done.14, bf16[32,192,128]{2,1,0:T(8,128)(2,1)S(1)} %all_to_all.21.got_ref), custom_call_target="tpu_custom_call" | custom-call | flops 3145728 | bytes 3145728 | tf_op jit(solution)/shard_map/pallas_call | solution.py:353
  120.7 4.8 %all-to-all-start.3 = ((bf16[32,192,128]{2,1,0:T(8,128)(2,1)}), bf16[32,192,128]{2,1,0:T(8,128)(2,1)S(1)}, u32[]{:S(2)}, u32[]{:S(2)}) async-start(bf16[32,192,128]{2,1,0:T(8,128)(2,1)} %shard_map.135), calls=%async_computation.3 | async-start | bytes 3145728 | tf_op jit(solution)/shard_map/all_to_all | solution.py:249
  125.6 2.0 %collective-permute-start.2 = (bf16[256,128]{1,0:T(8,128)(2,1)}, bf16[256,128]{1,0:T(8,128)(2,1)S(1)}, u32[]{:S(2)}, u32[]{:S(2)}) collective-permute-start(bf16[256,128]{1,0:T(8,128)(2,1)} %get-tuple-element.16), channel_id=1, source_target_pairs={{0,1},{1,2},{2,3},{4,5},{5,6},{6,7},{8,9},{9,10},{10,11},{12,13},{... | collective-permute-start | bytes 196616 | tf_op jit(solution)/shard_map/ppermute | solution.py:245
  127.6 1.3 collective-permute-start.3
  128.9 0.0 copy-start.3
  128.9 2.8 %copy-done.3 = bf16[3,1,8,8,128,128]{5,4,3,2,1,0:T(8,128)(2,1)S(1)} copy-done((bf16[3,1,8,8,128,128]{5,4,3,2,1,0:T(8,128)(2,1)S(1)}, bf16[3,1,8,8,128,128]{5,4,3,2,1,0:T(8,128)(2,1)}, u32[]{:S(2)}) %copy-start.3) | copy-done | bytes 6291480
  131.7 2.2 %shard_map.136.local_ref = f32[3,256,128]{2,1,0:T(8,128)S(1)} custom-call(s32[3]{0:T(128)S(1)} %broadcast_subtract_fusion.remaining_ref, f32[3,256,128]{2,1,0:T(8,128)S(1)} %get-tuple-element.15.field_ref, f32[3,256,128]{2,1,0:T(8,128)S(1)} %get-tuple-element.11.field_ref.prev_ref, bf16[3,1,8,8,128,128]{5,4,3,2,1,0:T(8,128)(2,1)S(1)} %copy-done.3, ...), custom_call_target="tpu_custom_call" | custom-call | flops 402653184 | bytes 393216 | tf_op jit(solution)/shard_map/pallas_call | solution.py:350
  133.9 0.0 collective-permute-done.2.below_ref
  133.9 0.0 collective-permute-done.3.above_ref
  134.0 16.0 %all-to-all-done.3.got_ref = bf16[32,192,128]{2,1,0:T(8,128)(2,1)S(1)} async-done(((bf16[32,192,128]{2,1,0:T(8,128)(2,1)}), bf16[32,192,128]{2,1,0:T(8,128)(2,1)S(1)}, u32[]{:S(2)}, u32[]{:S(2)}) %all-to-all-start.3) | async-done | bytes 1572896 | tf_op jit(solution)/shard_map/all_to_all | solution.py:249
  149.9 2.8 %copy-done.4 = bf16[3,1,8,8,128,128]{5,4,3,2,1,0:T(8,128)(2,1)S(1)} copy-done((bf16[3,1,8,8,128,128]{5,4,3,2,1,0:T(8,128)(2,1)S(1)}, bf16[3,1,8,8,128,128]{5,4,3,2,1,0:T(8,128)(2,1)}, u32[]{:S(2)}) %copy-start.4) | copy-done | bytes 6291480
  152.7 4.2 %shard_map.137 = (f32[3,128,256]{2,1,0:T(8,128)}, f32[3,128,256]{2,1,0:T(8,128)}) custom-call(s32[3]{0:T(128)S(1)} %broadcast_subtract_fusion.remaining_ref, bf16[32,192,128]{2,1,0:T(8,128)(2,1)S(1)} %all-to-all-done.3.got_ref, f32[3,256,128]{2,1,0:T(8,128)S(1)} %shard_map.136.local_ref, bf16[3,1,8,8,128,128]{5,4,3,2,1,0:T(8,128)(2,1)S(1)} %copy-done.4, ...), custom_call_target="tpu_custom_call" | custom-call | flops 1409286144 | bytes 6291456 | tf_op jit(solution)/shard_map/pallas_call | solution.py:359
  (15 shorter events, 0.0 us)
Async XLA Ops:
  2.1 2.8 %copy-start = (bf16[3,1,8,8,128,128]{5,4,3,2,1,0:T(8,128)(2,1)S(1)}, bf16[3,1,8,8,128,128]{5,4,3,2,1,0:T(8,128)(2,1)}, u32[]{:S(2)}) copy-start(bf16[3,1,8,8,128,128]{5,4,3,2,1,0:T(8,128)(2,1)} %blocks_ref.5) | copy-start | bytes 18874372
  4.9 1.0 copy-start.9
  5.9 0.7 copy-start.10
  11.1 34.7 %copy-start.14 = (s32[3,7]{1,0:T(4,128)S(1)}, s32[3,7]{1,0:T(4,128)}, u32[]{:S(2)}) copy-start(s32[3,7]{1,0:T(4,128)} %offsets_ref.3) | copy-start | bytes 256
  49.5 7.2 %copy-start.5 = (f32[256,128]{1,0:T(8,128)S(1)}, f32[256,128]{1,0:T(8,128)}, u32[]{:S(2)}) copy-start(f32[256,128]{1,0:T(8,128)} %constant.16.clone.rest_3_.damp_ref) | copy-start | bytes 393220
  49.5 7.2 %copy-start.6 = (f32[256,128]{1,0:T(8,128)S(1)}, f32[256,128]{1,0:T(8,128)}, u32[]{:S(2)}) copy-start(f32[256,128]{1,0:T(8,128)} %constant.15.clone.rest_2_.cent_ref) | copy-start | bytes 393220
  49.5 7.3 %copy-start.7 = (f32[256,256]{1,0:T(8,128)S(1)}, f32[256,256]{1,0:T(8,128)}, u32[]{:S(2)}) copy-start(f32[256,256]{1,0:T(8,128)} %constant.14.clone.rest_1_) | copy-start | bytes 786436
  49.5 7.3 %copy-start.8 = (f32[3,128,256]{2,1,0:T(8,128)S(1)}, f32[3,128,256]{2,1,0:T(8,128)}, u32[]{:S(2)}) copy-start(f32[3,128,256]{2,1,0:T(8,128)} %prev_ref.1) | copy-start | bytes 1179652
  49.5 7.3 %copy-start.11 = (f32[3,128]{1,0:T(4,128)S(1)}, f32[3,128]{1,0:T(4,128)}, u32[]{:S(2)}) copy-start(f32[3,128]{1,0:T(4,128)} %cor_ref.5) | copy-start | bytes 4612
  49.6 7.3 %copy-start.12 = (f32[3,128]{1,0:T(4,128)S(1)}, f32[3,128]{1,0:T(4,128)}, u32[]{:S(2)}) copy-start(f32[3,128]{1,0:T(4,128)} %rest_4_.3) | copy-start | bytes 4612
  49.6 7.3 %copy-start.13 = (f32[3,128]{1,0:T(4,128)S(1)}, f32[3,128]{1,0:T(4,128)}, u32[]{:S(2)}) copy-start(f32[3,128]{1,0:T(4,128)} %rest_5_.3) | copy-start | bytes 4612
  49.6 27.3 %all-to-all-start.1 = ((bf16[32,192,128]{2,1,0:T(8,128)(2,1)}), bf16[32,192,128]{2,1,0:T(8,128)(2,1)S(1)}, u32[]{:S(2)}, u32[]{:S(2)}) async-start(bf16[32,192,128]{2,1,0:T(8,128)(2,1)} %shard_map.132), calls=%async_computation.1 | async-start | bytes 3145728 | tf_op jit(solution)/shard_map/all_to_all | solution.py:249
  54.2 7.7 %collective-permute-start = (bf16[256,128]{1,0:T(8,128)(2,1)}, bf16[256,128]{1,0:T(8,128)(2,1)S(1)}, u32[]{:S(2)}, u32[]{:S(2)}) collective-permute-start(bf16[256,128]{1,0:T(8,128)(2,1)} %get-tuple-element.12), channel_id=1, source_target_pairs={{0,1},{1,2},{2,3},{4,5},{5,6},{6,7},{8,9},{9,10},{10,11},{12,13},{... | collective-permute-start | bytes 196616 | tf_op jit(solution)/shard_map/ppermute | solution.py:245
  55.5 7.1 %collective-permute-start.1 = (bf16[256,128]{1,0:T(8,128)(2,1)}, bf16[256,128]{1,0:T(8,128)(2,1)S(1)}, u32[]{:S(2)}, u32[]{:S(2)}) collective-permute-start(bf16[256,128]{1,0:T(8,128)(2,1)} %get-tuple-element.13), channel_id=1, source_target_pairs={{1,0},{2,1},{3,2},{5,4},{6,5},{7,6},{9,8},{10,9},{11,10},{13,12},{... | collective-permute-start | bytes 196616 | tf_op jit(solution)/shard_map/ppermute | solution.py:245
  56.8 2.8 %copy-start.1 = (bf16[3,1,8,8,128,128]{5,4,3,2,1,0:T(8,128)(2,1)S(1)}, bf16[3,1,8,8,128,128]{5,4,3,2,1,0:T(8,128)(2,1)}, u32[]{:S(2)}) copy-start(bf16[3,1,8,8,128,128]{5,4,3,2,1,0:T(8,128)(2,1)} %blocks_ref.5) | copy-start | bytes 18874372
  61.9 0.6 copy-start.16
  62.5 0.6 copy-start.18
  76.8 2.8 %copy-start.2 = (bf16[3,1,8,8,128,128]{5,4,3,2,1,0:T(8,128)(2,1)S(1)}, bf16[3,1,8,8,128,128]{5,4,3,2,1,0:T(8,128)(2,1)}, u32[]{:S(2)}) copy-start(bf16[3,1,8,8,128,128]{5,4,3,2,1,0:T(8,128)(2,1)} %blocks_ref.5) | copy-start | bytes 18874372
  79.6 0.8 copy-start.17
  80.5 0.8 copy-start.19
  88.2 32.6 %copy-start.15 = (bf16[256,128]{1,0:T(8,128)(2,1)}, bf16[256,128]{1,0:T(8,128)(2,1)S(1)}, u32[]{:S(2)}) copy-start(bf16[256,128]{1,0:T(8,128)(2,1)S(1)} %get-tuple-element.17) | copy-start | bytes 196612
  120.7 29.2 %all-to-all-start.3 = ((bf16[32,192,128]{2,1,0:T(8,128)(2,1)}), bf16[32,192,128]{2,1,0:T(8,128)(2,1)S(1)}, u32[]{:S(2)}, u32[]{:S(2)}) async-start(bf16[32,192,128]{2,1,0:T(8,128)(2,1)} %shard_map.135), calls=%async_computation.3 | async-start | bytes 3145728 | tf_op jit(solution)/shard_map/all_to_all | solution.py:249
  125.6 8.3 %collective-permute-start.2 = (bf16[256,128]{1,0:T(8,128)(2,1)}, bf16[256,128]{1,0:T(8,128)(2,1)S(1)}, u32[]{:S(2)}, u32[]{:S(2)}) collective-permute-start(bf16[256,128]{1,0:T(8,128)(2,1)} %get-tuple-element.16), channel_id=1, source_target_pairs={{0,1},{1,2},{2,3},{4,5},{5,6},{6,7},{8,9},{9,10},{10,11},{12,13},{... | collective-permute-start | bytes 196616 | tf_op jit(solution)/shard_map/ppermute | solution.py:245
  127.6 6.4 %collective-permute-start.3 = (bf16[256,128]{1,0:T(8,128)(2,1)}, bf16[256,128]{1,0:T(8,128)(2,1)S(1)}, u32[]{:S(2)}, u32[]{:S(2)}) collective-permute-start(bf16[256,128]{1,0:T(8,128)(2,1)} %copy-done.15), channel_id=1, source_target_pairs={{1,0},{2,1},{3,2},{5,4},{6,5},{7,6},{9,8},{10,9},{11,10},{13,12},{... | collective-permute-start | bytes 196616 | tf_op jit(solution)/shard_map/ppermute | solution.py:245
  128.9 2.8 %copy-start.3 = (bf16[3,1,8,8,128,128]{5,4,3,2,1,0:T(8,128)(2,1)S(1)}, bf16[3,1,8,8,128,128]{5,4,3,2,1,0:T(8,128)(2,1)}, u32[]{:S(2)}) copy-start(bf16[3,1,8,8,128,128]{5,4,3,2,1,0:T(8,128)(2,1)} %blocks_ref.5) | copy-start | bytes 18874372
  149.9 2.8 %copy-start.4 = (bf16[3,1,8,8,128,128]{5,4,3,2,1,0:T(8,128)(2,1)S(1)}, bf16[3,1,8,8,128,128]{5,4,3,2,1,0:T(8,128)(2,1)}, u32[]{:S(2)}) copy-start(bf16[3,1,8,8,128,128]{5,4,3,2,1,0:T(8,128)(2,1)} %blocks_ref.5) | copy-start | bytes 18874372

commit v2 on v0

v2 whole, which is shorter than its diff:
```python
import functools

import jax
import jax.numpy as jnp
import numpy as np
from jax import lax
from jax.experimental import pallas as pl
from jax.experimental.pallas import tpu as pltpu
from jax.sharding import PartitionSpec as P

STEPS = 2
BF = jnp.bfloat16
F32 = jnp.float32
VMEM_LIMIT = 24 * 1024 * 1024
SIDES = 7


def kinetic_matrix(points):
    n = points + 1
    i = np.arange(1, n, dtype=np.float64)[:, None]
    k = i.T
    gap = np.where(i == k, 1.0, i - k)
    parity = 1.0 - 2.0 * (np.abs(i - k) % 2)
    off = parity * (1.0 / np.sin(np.pi * gap / (2 * n)) ** 2 - 1.0 / np.sin(np.pi * (i + k) / (2 * n)) ** 2)
    diagonal = (2.0 * n * n + 1.0) / 3.0 - 1.0 / np.sin(np.pi * i / n) ** 2
    return (np.where(i == k, diagonal, off) * (0.25 / (n * n))).astype(np.float32)


def radial_profiles(points, width):
    r = np.arange(points, dtype=np.float64)
    centrifugal = 0.1 / (1.0 + 8.0 * r / points) ** 2
    damping = np.exp(-0.002 * np.maximum(r - 3 * points // 4, 0.0) ** 2)
    spread = lambda v: np.ascontiguousarray(np.broadcast_to(v.astype(np.float32)[:, None], (points, width)))
    return spread(centrifugal), spread(damping)


def dot_nn(a, b):
    return lax.dot_general(a, b, (((1,), (0,)), ((), ())), preferred_element_type=F32)


def dot_nt(a, b):
    return lax.dot_general(a, b, (((1,), (1,)), ((), ())), preferred_element_type=F32)


def active_row(counts_ref, h, width):
    channel = lax.axis_index("chan") * width + lax.broadcasted_iota(jnp.int32, (1, width), 1)
    return (channel < counts_ref[h]).astype(F32)


def radial_columns(radial_ref, shape):
    columns = radial_ref[...].T
    return [jnp.broadcast_to(columns[:, l : l + 1], shape) for l in range(columns.shape[1])]


def weight(wide, columns):
    return jnp.concatenate([(wide * column).astype(BF) for column in columns], axis=1)


def interleave(a, b, count):
    pieces = (count, -1, a.shape[1])
    return jnp.concatenate([a.reshape(pieces), b.reshape(pieces)], axis=1).astype(BF)


def emit_products(field, blocks_ref, columns, send_ref, arrived=None):
    width = field.shape[1]
    count, rows = send_ref.shape[:2]
    pair = rows // 4
    wide = field.astype(BF).astype(F32)
    weighted = jnp.concatenate([(wide * column).astype(BF) for column in columns], axis=1)
    if arrived is not None:
        arrived()
    send_ref[:, :pair, :] = interleave(wide, dot_nn(weighted, blocks_ref[0].reshape(-1, width)), count)
    for p in range(1, 4):
        rhs = [blocks_ref[j].reshape(-1, width) for j in (2 * p - 1, 2 * p)]
        out = dot_nn(weighted, jnp.concatenate(rhs, axis=1))
        send_ref[:, p * pair : (p + 1) * pair, :] = interleave(out[:, :width], out[:, width:], count)


def fetch(blocks_ref, kept_ref, sem):
    copies = []
    for h in range(blocks_ref.shape[0]):
        copies.append([])
        for k, at in enumerate(range(0, SIDES, 2)):
            size = min(2, SIDES - at)
            source = blocks_ref.at[h, 0, pl.ds(1 + at, size)]
            copies[h].append(pltpu.make_async_copy(source, kept_ref.at[h, pl.ds(at, size)], sem.at[h, k]))
            copies[h][-1].start()

    def arrive(h):
        for copy in copies[h]:
            copy.wait()

    return [functools.partial(arrive, h) for h in range(len(copies))]


def emit_edges(h, field, cor_ref, up_ref, down_ref):
    last = cor_ref.shape[0] - 1
    if h == last:
        up_ref[...] = (field * cor_ref[last : last + 1, :]).astype(BF)
    if h == 0:
        down_ref[...] = field.astype(BF)


def copy_out(h, made_ref, send_ref, sem):
    rows = made_ref.shape[2]
    copy = pltpu.make_async_copy(made_ref.at[h], send_ref.at[:, pl.ds(h * rows, rows), :], sem.at[h])
    copy.start()
    return copy


def first_kernel(
    counts_ref, radial_ref, cor_ref, psi_ref, blocks_ref, field_ref, up_ref, down_ref, send_ref,
    here_ref, kept_ref, made_ref, psi_sem, block_sem, send_sem,
):
    helicities, _, width = field_ref.shape
    psi = [pltpu.make_async_copy(psi_ref.at[h], here_ref.at[h], psi_sem.at[h]) for h in range(helicities)]
    psi[0].start()
    arrived = fetch(blocks_ref, kept_ref, block_sem)
    for copy in psi[1:]:
        copy.start()
    columns = radial_columns(radial_ref, field_ref.shape[1:])
    sent = []
    for h in range(helicities):
        psi[h].wait()
        field = here_ref[h].T * active_row(counts_ref, h, width)
        field_ref[h] = field
        emit_edges(h, field, cor_ref, up_ref, down_ref)
        emit_products(field, kept_ref.at[h], columns, made_ref.at[h], arrived[h])
        sent.append(copy_out(h, made_ref, send_ref, send_sem))
    for copy in sent:
        copy.wait()


def route_kernel(offsets_ref, got_ref, *refs):
    send_ref, wide_ref = refs[-2:]
    count = got_ref.shape[0]
    helicities = offsets_ref.shape[0]
    rows = got_ref.shape[1] // helicities
    piece = rows // (1 + SIDES)
    for h in range(helicities):
        mine = slice(h * rows, (h + 1) * rows)

        def widen(i, carry):
            for u in range(4):
                wide = got_ref[4 * i + u, mine, :].astype(F32)
                wide_ref[4 * i + u] = wide
                wide_ref[4 * i + u + count] = wide
            return carry

        lax.fori_loop(0, count // 4, widen, 0)
        ahead = [wide_ref.at[pl.ds(offsets_ref[h, j], count)] for j in range(SIDES)]
        behind = [wide_ref.at[pl.ds(count - offsets_ref[h, j], count)] for j in range(SIDES)]
        for d in range(count):
            out = [ref[d, :piece, :] for ref in ahead]
            terms = [ref[d, (1 + j) * piece : (2 + j) * piece, :] for j, ref in enumerate(behind)]
            while len(terms) > 1:
                terms = [sum(terms[k + 1 : k + 2], terms[k]) for k in range(0, len(terms), 2)]
            send_ref[d, mine, :] = jnp.concatenate(out + terms, axis=0).astype(BF)


def forward(sources, blocks, columns, total, arrived=None):
    points, width = total.shape
    terms = blocks[0].shape[0]
    sources = jnp.concatenate(sources, axis=1)
    if arrived is not None:
        arrived()
    for l in range(0, terms, 2):
        rhs = jnp.concatenate([jnp.concatenate([b[l + u] for b in blocks], axis=1) for u in range(2)], axis=0)
        out = dot_nt(sources, rhs)
        for u in range(2):
            total = total + columns[l + u] * out[:, u * width : (u + 1) * width]
    return total


def local_kernel(
    final, counts_ref, prev_ref, radial_ref, kin_ref, cent_ref, damp_ref, e_ref, rot_ref, cor_ref, field_ref, blocks_ref, out_ref, *refs
):
    helicities, points, width = field_ref.shape
    terms = blocks_ref.shape[3]
    cent = cent_ref[...]
    damp = damp_ref[...]
    columns = radial_columns(radial_ref, (points, width))
    for h in range(helicities):
        mask = active_row(counts_ref, h, width)
        field = field_ref[h]
        half = field.astype(BF)
        total = lax.dot_general(
            kin_ref[...], field, (((1,), (0,)), ((), ())), precision=lax.Precision.HIGHEST, preferred_element_type=F32
        )
        for l in range(terms):
            total = total + columns[l] * dot_nn(half, blocks_ref[h, 0, 0, l])
        total = forward([half], [blocks_ref.at[h, 0, 0]], columns, total)
        total = total + (e_ref[h : h + 1, :] + cent * rot_ref[h : h + 1, :]) * field
        if h + 1 < helicities:
            total = total - cent * (cor_ref[h : h + 1, :] * field_ref[h + 1])
        if h > 0:
            total = total - cent * (cor_ref[h - 1 : h, :] * field_ref[h - 1])
        previous = prev_ref[h] if final else prev_ref[h].T * mask
        out_ref[h] = damp * (2.0 * (mask * total) - damp * previous)
        if final:
            refs[0][h] = field.T


def renew(h, got_ref, counts_ref, local_ref, columns, cent_ref, damp_ref, cor_ref, below_ref, above_ref, kept_ref, arrived):
    helicities, points, width = local_ref.shape
    rows = got_ref.shape[1] // helicities
    pair = rows // 4
    slots = []
    for p in range(4):
        both = got_ref[:, h * rows + p * pair : h * rows + (p + 1) * pair, :].astype(F32)
        slots += [both[:, : pair // 2].reshape(points, width), both[:, pair // 2 :].reshape(points, width)]
    total = slots[-1]
    if h == 0:
        total = total - cent_ref[...] * below_ref[...].astype(F32)
    if h == helicities - 1:
        total = total - cent_ref[...] * (above_ref[...].astype(F32) * cor_ref[h : h + 1, :])
    sources = [slot.astype(BF) for slot in slots[:-1]]
    total = forward(sources, [kept_ref.at[h, j] for j in range(SIDES)], columns, total, arrived[h])
    return local_ref[h] + 2.0 * damp_ref[...] * (active_row(counts_ref, h, width) * total)


def middle_kernel(
    counts_ref, radial_ref, cent_ref, damp_ref, cor_ref, got_ref, local_ref, below_ref, above_ref, blocks_ref,
    field_ref, up_ref, down_ref, send_ref, kept_ref, made_ref, block_sem, send_sem,
):
    arrived = fetch(blocks_ref, kept_ref, block_sem)
    columns = radial_columns(radial_ref, local_ref.shape[1:])
    sent = []
    for h in range(local_ref.shape[0]):
        field = renew(
            h, got_ref, counts_ref, local_ref, columns, cent_ref, damp_ref, cor_ref, below_ref, above_ref, kept_ref, arrived
        )
        field_ref[h] = field
        emit_edges(h, field, cor_ref, up_ref, down_ref)
        emit_products(field, kept_ref.at[h], columns, made_ref.at[h])
        sent.append(copy_out(h, made_ref, send_ref, send_sem))
    for copy in sent:
        copy.wait()


def last_kernel(
    counts_ref, radial_ref, cent_ref, damp_ref, cor_ref, got_ref, local_ref, below_ref, above_ref, blocks_ref, out_ref,
    kept_ref, made_ref, block_sem, sem,
):
    arrived = fetch(blocks_ref, kept_ref, block_sem)
    columns = radial_columns(radial_ref, local_ref.shape[1:])
    sent = []
    for h in range(local_ref.shape[0]):
        field = renew(
            h, got_ref, counts_ref, local_ref, columns, cent_ref, damp_ref, cor_ref, below_ref, above_ref, kept_ref, arrived
        )
        made_ref[h] = field.T
        copy = pltpu.make_async_copy(made_ref.at[h], out_ref.at[h], sem.at[h])
        copy.start()
        sent.append(copy)
    for copy in sent:
        copy.wait()


def shifted(x, axis, by):
    peers = lax.axis_size(axis)
    return lax.ppermute(x, axis, [(i, i + by) for i in range(peers) if 0 <= i + by < peers])


def exchange(x):
    return lax.all_to_all(x, "chan", 0, 0, tiled=True)


def body(psi_prev, psi_cur, blocks, radial_terms, energies, rotation, coriolis, counts, offsets):
    helicities, width, points = psi_cur.shape
    count = lax.axis_size("chan")
    terms = blocks.shape[3]
    rows = (1 + SIDES) * points // count
    assert blocks.shape[2] == offsets.shape[1] + 1 == SIDES + 1
    kinetic = jnp.asarray(kinetic_matrix(points))
    cent, damp = (jnp.asarray(v) for v in radial_profiles(points, width))

    smem = pl.BlockSpec(memory_space=pltpu.SMEM)
    vmem = pl.BlockSpec(memory_space=pltpu.VMEM)
    hbm = pl.BlockSpec(memory_space=pl.ANY)
    whole = lambda a: pl.BlockSpec(a.shape, lambda *_: (0,) * a.ndim)
    place = lambda a: pltpu.with_memory_space_constraint(a, pltpu.HBM)
    psi_cur, psi_prev, blocks, radial_terms, counts, offsets = map(
        place, (psi_cur, psi_prev, blocks, radial_terms, counts, offsets)
    )

    field_shape = (helicities, points, width)
    field_out = pltpu.VMEM(field_shape, F32)
    parcel_shape = (count, helicities * rows, width)
    parcel_out = pltpu.HBM(parcel_shape, BF)
    edge_out = pltpu.HBM((points, width), BF)
    edge = pl.BlockSpec(edge_out.shape, lambda *_: (0, 0))
    made = pltpu.VMEM((helicities, count, rows, width), BF)
    kept = pltpu.VMEM((helicities, SIDES) + blocks.shape[3:], BF)
    copies = pltpu.SemaphoreType.DMA((helicities,))
    parts = pltpu.SemaphoreType.DMA((helicities, (SIDES + 1) // 2))
    diagonal = pl.BlockSpec((helicities, 1, 1) + blocks.shape[3:], lambda *_: (0,) * blocks.ndim)
    mac = 2 * helicities * points * width * width * terms

    def call(kernel, in_specs, out_specs, out_shape, flops, moved, scratch=()):
        return pl.pallas_call(
            kernel,
            grid=(1,),
            in_specs=in_specs,
            out_specs=out_specs,
            out_shape=out_shape,
            scratch_shapes=scratch,
            compiler_params=pltpu.CompilerParams(vmem_limit_bytes=VMEM_LIMIT),
            cost_estimate=pl.CostEstimate(flops=flops, bytes_accessed=moved, transcendentals=0),
        )

    first = call(
        first_kernel,
        [smem, whole(radial_terms), whole(coriolis), hbm, hbm],
        [vmem, edge, edge, hbm],
        [field_out, edge_out, edge_out, parcel_out],
        SIDES * mac,
        blocks.size * 2,
        [pltpu.VMEM(psi_cur.shape, F32), kept, made, copies, parts, copies],
    )
    route = call(
        route_kernel,
        [smem, vmem, hbm, hbm, hbm],
        vmem,
        pltpu.VMEM(parcel_shape, BF),
        psi_cur.size * 8,
        psi_cur.size * 4,
        [pltpu.VMEM((2 * count, rows, width), F32)],
    )

    def local(final):
        kernel = functools.partial(local_kernel, final)
        tables = [whole(a) for a in (psi_prev, radial_terms, kinetic, cent, damp, energies, rotation, coriolis)]
        if final:
            tables[0] = vmem
        out_specs = [vmem, whole(psi_prev)] if final else vmem
        out_shape = [field_out, pltpu.HBM(psi_prev.shape, F32)] if final else field_out
        return call(kernel, [smem] + tables + [vmem, diagonal], out_specs, out_shape, 2 * mac, 4 * psi_cur.size)

    given = [smem, *[whole(a) for a in (radial_terms, cent, damp, coriolis)], vmem, vmem, edge, edge, hbm]
    middle = call(
        middle_kernel,
        given,
        [vmem, edge, edge, hbm],
        [field_out, edge_out, edge_out, parcel_out],
        2 * SIDES * mac,
        blocks.size,
        [kept, made, parts, copies],
    )
    final = call(
        last_kernel,
        given,
        hbm,
        pltpu.HBM(psi_cur.shape, F32),
        SIDES * mac,
        blocks.size,
        [kept, pltpu.VMEM(psi_cur.shape, F32), parts, copies],
    )

    field, up, down, send = first(counts, radial_terms, coriolis, psi_cur, blocks)
    prev = psi_prev
    for iteration in range(STEPS):
        ends = iteration + 1 == STEPS
        got = exchange(send)
        below = shifted(up, "hel", 1)
        above = shifted(down, "hel", -1)
        rest = local(iteration > 0)(
            counts, prev, radial_terms, kinetic, cent, damp, energies, rotation, coriolis, field, blocks
        )
        if ends:
            rest, before = rest
        back = exchange(route(offsets, got, rest, below, above))
        given = (counts, radial_terms, cent, damp, coriolis, back, rest, below, above, blocks)
        if ends:
            return before, final(*given)
        prev = field
        field, up, down, send = middle(*given)


def solution(mesh):
    in_specs = (
        P("hel", "chan", None),
        P("hel", "chan", None),
        P("hel", "chan", None, None, None, None),
        P(),
        P("hel", "chan"),
        P("hel", "chan"),
        P("hel", "chan"),
        P("hel"),
        P("hel", None),
    )
    out_specs = (P("hel", "chan", None), P("hel", "chan", None))
    return jax.shard_map(body, mesh=mesh, in_specs=in_specs, out_specs=out_specs, check_vma=False)
```

time: 695 us -> 147 us (0.21); the launches traced: 686 us -> 147 us
  waiting for transfers between devices: 561 us -> 34.9 us
  matrix products: 63 us -> 0 us
  blocking collectives: 0 us -> 57.2 us
  local copies, waits for them, and re-layouts: 33.3 us -> 0.74 us
  Pallas kernels: 0 us -> 30.9 us
  starting transfers between devices: 5.94 us -> 21.9 us
  between operations: 14.9 us -> 1.06 us
  other arithmetic: 8.11 us -> 0 us
    reduce_scatter x2 -> x0, waiting for transfers between devices: 440 us -> none  [body(): lax.psum_scatter(jnp.einsum('qhj,hjdr->qhdr', slot_mask, products, precis...]
    all_gather x2 -> x0, waiting for transfers between devices: 119 us -> none  [body(): shard_piece = lax.all_gather(psi_half, 'chan', axis=1, tiled=True)]
    dot_general x14 -> x0, matrix products: 63 us -> none  [the longest x2 13.5 us: body(): jnp.einsum('hjlcd,lhjdr->hcr', side_blocks, remote_weighted, preferred_el...]
    all_to_all x0 -> x2, blocking collectives: none -> 57.2 us  [exchange(): return lax.all_to_all(x, 'chan', 0, 0, tiled=True)]
    all_to_all x0 -> x2, waiting for transfers between devices: none -> 34.9 us  [exchange(): return lax.all_to_all(x, 'chan', 0, 0, tiled=True)]
    pallas_call x0 -> x7, Pallas kernels: none -> 30.9 us  [the longest x1 8.28 us: body(): field, up, down, send = middle(*given)]
    dot_general x6 -> x0, local copies, waits for them, and re-layouts: 20 us -> none  [the longest x2 12.5 us: body(): jnp.einsum('qhj,hjdr->qhdr', slot_mask, products, precision=lax.Precision...]
    all_to_all x0 -> x2, starting transfers between devices: none -> 15.8 us  [exchange(): return lax.all_to_all(x, 'chan', 0, 0, tiled=True)]
  transfers between devices with their start and end apart: 8 -> 6, of which waited for: 5 -> 2; matrix products, arithmetic and copies ran while one was open for 12% -> 0% of each run, Pallas kernels for 0% -> 5%
where the time goes in v2:
time: 147 us
  blocking collectives  57.2 us (39%)
  waiting for transfers between devices  34.9 us (24%)
  Pallas kernels  30.9 us (21%)
  starting transfers between devices  21.9 us (15%)
    all_to_all x2, blocking collectives, exchange(): return lax.all_to_all(x, 'chan', 0, 0, tiled=True)  57.2 us
    all_to_all x2, waiting for transfers between devices, exchange(): return lax.all_to_all(x, 'chan', 0, 0, tiled=True)  34.9 us
    all_to_all x2, starting transfers between devices, exchange(): return lax.all_to_all(x, 'chan', 0, 0, tiled=True)  15.8 us
    pallas_call x1, Pallas kernels, body(): field, up, down, send = middle(*given)  8.28 us
    pallas_call x1, Pallas kernels, body(): first(counts, radial_terms, coriolis, psi_cur, blocks)  7.04 us
    pallas_call x2, Pallas kernels, body(): local(iteration > 0)  6.81 us
    ppermute x4, starting transfers between devices, shifted(): lax.ppermute(x, axis, [(i, i + by) for i in range(peers) if 0 <= i + by <...  6.08 us
    pallas_call x1, Pallas kernels, body(): return (before, final(*given))  5.53 us
  transfers between devices with their start and end apart: 6, of which 2 were waited for; matrix products, arithmetic and copies ran while one was open for 0% of the time, Pallas kernels for 5%

profile of v2, /device:TPU:0, one launch (start us, length us, event | category | flops | bytes accessed | tf_op | source)
XLA Modules:
  0.0 146.7 jit_solution(10060672071024422420)
XLA Ops:
  0.6 0.0 copy-start.3
  0.6 0.7 copy-done.3
  1.3 7.0 %shard_map.131 = (f32[3,256,128]{2,1,0:T(8,128)S(1)}, bf16[256,128]{1,0:T(8,128)(2,1)}, bf16[256,128]{1,0:T(8,128)(2,1)}, bf16[32,192,128]{2,1,0:T(8,128)(2,1)}) custom-call(s32[3]{0:T(128)} %counts_ref.9, f32[8,256]{1,0:T(8,128)} %radial_ref.9, f32[3,128]{1,0:T(4,128)S(1)} %copy-done.3, f32[3,128,256]{2,1,0:T(8,128)} %psi_ref.1, ...), custom_call_target="tpu_custom_call" | custom-call | flops 1409286144 | bytes 6291456 | tf_op jit(solution)/shard_map/pallas_call | solution.py:360
  8.4 0.0 copy-start.10
  8.4 0.0 copy-start.9
  8.4 0.0 copy-start
  8.4 0.0 copy-start.1
  8.4 0.0 copy-start.2
  8.4 0.0 copy-start.4
  8.4 0.0 copy-start.5
  8.4 0.0 copy-start.6
  8.5 10.9 %all-to-all-start = ((bf16[32,192,128]{2,1,0:T(8,128)(2,1)}), bf16[32,192,128]{2,1,0:T(8,128)(2,1)S(1)}, u32[]{:S(2)}, u32[]{:S(2)}) async-start(bf16[32,192,128]{2,1,0:T(8,128)(2,1)} %get-tuple-element.13), calls=%async_computation | async-start | bytes 3145728 | tf_op jit(solution)/shard_map/all_to_all | solution.py:266
  19.3 0.0 copy-done.10
  19.3 1.5 collective-permute-start
  20.8 0.0 copy-done.9
  20.8 1.3 collective-permute-start.1
  22.1 0.0 copy-done
  22.1 0.0 copy-done.1
  22.1 0.0 copy-done.2
  22.1 0.0 copy-done.4
  22.2 0.0 copy-done.5
  22.2 0.0 copy-done.6
  22.2 3.1 %shard_map.132.refs_0_.local_ref = f32[3,256,128]{2,1,0:T(8,128)S(1)} custom-call(s32[3]{0:T(128)} %counts_ref.9, f32[3,128,256]{2,1,0:T(8,128)} %prev_ref.1, f32[8,256]{1,0:T(8,128)} %radial_ref.9, f32[256,256]{1,0:T(8,128)S(1)} %copy-done.2, f32[256,128]{1,0:T(8,128)S(1)} %copy-done.1, f32[256,128]{1,0:T(8,128)S(1)} %copy-done, f32[3,128]{1,0:T(4,128)S(1)} %copy-done.5, ...), custom_call_target="tpu_custom_call" | custom-call | flops 402653184 | bytes 393216 | tf_op jit(solution)/shard_map/pallas_call | solution.py:367
  25.3 0.0 collective-permute-done.refs_1_.below_ref
  25.3 0.0 collective-permute-done.1.refs_2_.above_ref
  25.3 17.8 %all-to-all-done.got_ref = bf16[32,192,128]{2,1,0:T(8,128)(2,1)S(1)} async-done(((bf16[32,192,128]{2,1,0:T(8,128)(2,1)}), bf16[32,192,128]{2,1,0:T(8,128)(2,1)S(1)}, u32[]{:S(2)}, u32[]{:S(2)}) %all-to-all-start) | async-done | bytes 1572896 | tf_op jit(solution)/shard_map/all_to_all | solution.py:266
  43.1 1.6 %shard_map.133 = bf16[32,192,128]{2,1,0:T(8,128)(2,1)S(1)} custom-call(s32[3,7]{1,0:T(4,128)} %offsets_ref.3, bf16[32,192,128]{2,1,0:T(8,128)(2,1)S(1)} %all-to-all-done.got_ref, f32[3,256,128]{2,1,0:T(8,128)S(1)} %shard_map.132.refs_0_.local_ref, bf16[256,128]{1,0:T(8,128)(2,1)S(1)} %collective-permute-done.refs_1_.below_ref, ...), custom_call_target="tpu_custom_call" | custom-call | flops 786432 | bytes 393216 | tf_op jit(solution)/shard_map/pallas_call | solution.py:372
  44.7 29.0 %all_to_all.20.got_ref = bf16[32,192,128]{2,1,0:T(8,128)(2,1)S(1)} all-to-all(bf16[32,192,128]{2,1,0:T(8,128)(2,1)S(1)} %shard_map.133), channel_id=1, replica_groups=mesh['chan'=32,'hel'=4] {'chan'}, dimensions={0} | all-to-all | bytes 3145728 | tf_op jit(solution)/shard_map/all_to_all | solution.py:266
  73.7 8.3 %shard_map.134 = (f32[3,256,128]{2,1,0:T(8,128)S(1)}, bf16[256,128]{1,0:T(8,128)(2,1)}, bf16[256,128]{1,0:T(8,128)(2,1)}, bf16[32,192,128]{2,1,0:T(8,128)(2,1)}) custom-call(s32[3]{0:T(128)} %counts_ref.9, f32[8,256]{1,0:T(8,128)} %radial_ref.9, f32[256,128]{1,0:T(8,128)S(1)} %copy-done.1, f32[256,128]{1,0:T(8,128)S(1)} %copy-done, f32[3,128]{1,0:T(4,128)S(1)} %copy-done.4, ...), custom_call_target="tpu_custom_call" | custom-call | flops 2818572288 | bytes 3145728 | tf_op jit(solution)/shard_map/pallas_call | solution.py:377
  82.0 0.0 copy-start.8
  82.0 0.0 copy-start.7
  82.0 5.0 %all-to-all-start.2 = ((bf16[32,192,128]{2,1,0:T(8,128)(2,1)}), bf16[32,192,128]{2,1,0:T(8,128)(2,1)S(1)}, u32[]{:S(2)}, u32[]{:S(2)}) async-start(bf16[32,192,128]{2,1,0:T(8,128)(2,1)} %get-tuple-element.18), calls=%async_computation.2 | async-start | bytes 3145728 | tf_op jit(solution)/shard_map/all_to_all | solution.py:266
  87.0 0.0 copy-done.8
  87.0 1.9 %collective-permute-start.2 = (bf16[256,128]{1,0:T(8,128)(2,1)S(1)}, bf16[256,128]{1,0:T(8,128)(2,1)S(1)}, u32[]{:S(2)}, u32[]{:S(2)}) collective-permute-start(bf16[256,128]{1,0:T(8,128)(2,1)S(1)} %copy-done.8), channel_id=1, source_target_pairs={{0,1},{1,2},{2,3},{4,5},{5,6},{6,7},{8,9},{9,10},{10,11},{12,13},{... | collective-permute-start | bytes 196616 | tf_op jit(solution)/shard_map/ppermute | solution.py:262
  88.9 0.0 copy-done.7
  88.9 1.5 %collective-permute-start.3 = (bf16[256,128]{1,0:T(8,128)(2,1)S(1)}, bf16[256,128]{1,0:T(8,128)(2,1)S(1)}, u32[]{:S(2)}, u32[]{:S(2)}) collective-permute-start(bf16[256,128]{1,0:T(8,128)(2,1)S(1)} %copy-done.7), channel_id=1, source_target_pairs={{1,0},{2,1},{3,2},{5,4},{6,5},{7,6},{9,8},{10,9},{11,10},{13,12},{... | collective-permute-start | bytes 196616 | tf_op jit(solution)/shard_map/ppermute | solution.py:262
  90.4 3.7 %shard_map.135 = (f32[3,256,128]{2,1,0:T(8,128)S(1)}, f32[3,128,256]{2,1,0:T(8,128)}) custom-call(s32[3]{0:T(128)} %counts_ref.9, f32[3,256,128]{2,1,0:T(8,128)S(1)} %get-tuple-element.12.field_ref.prev_ref, f32[8,256]{1,0:T(8,128)} %radial_ref.9, f32[256,256]{1,0:T(8,128)S(1)} %copy-done.2, f32[256,128]{1,0:T(8,128)S(1)} %copy-done.1, ...), custom_call_target="tpu_custom_call" | custom-call | flops 402653184 | bytes 393216 | tf_op jit(solution)/shard_map/pallas_call | solution.py:367
  94.1 0.0 collective-permute-done.2.refs_1_.below_ref
  94.1 0.0 collective-permute-done.3.refs_2_.above_ref
  94.1 17.1 %all-to-all-done.2.got_ref = bf16[32,192,128]{2,1,0:T(8,128)(2,1)S(1)} async-done(((bf16[32,192,128]{2,1,0:T(8,128)(2,1)}), bf16[32,192,128]{2,1,0:T(8,128)(2,1)S(1)}, u32[]{:S(2)}, u32[]{:S(2)}) %all-to-all-start.2) | async-done | bytes 1572896 | tf_op jit(solution)/shard_map/all_to_all | solution.py:266
  111.2 1.6 %shard_map.136 = bf16[32,192,128]{2,1,0:T(8,128)(2,1)S(1)} custom-call(s32[3,7]{1,0:T(4,128)} %offsets_ref.3, bf16[32,192,128]{2,1,0:T(8,128)(2,1)S(1)} %all-to-all-done.2.got_ref, f32[3,256,128]{2,1,0:T(8,128)S(1)} %get-tuple-element.19.refs_0_.local_ref, bf16[256,128]{1,0:T(8,128)(2,1)S(1)} %collective-permute-done.2.refs_1_.below_ref, ...), custom_call_target="tpu_custom_call" | custom-call | flops 786432 | bytes 393216 | tf_op jit(solution)/shard_map/pallas_call | solution.py:372
  112.8 28.2 %all_to_all.21.got_ref = bf16[32,192,128]{2,1,0:T(8,128)(2,1)S(1)} all-to-all(bf16[32,192,128]{2,1,0:T(8,128)(2,1)S(1)} %shard_map.136), channel_id=1, replica_groups=mesh['chan'=32,'hel'=4] {'chan'}, dimensions={0} | all-to-all | bytes 3145728 | tf_op jit(solution)/shard_map/all_to_all | solution.py:266
  141.0 5.5 %shard_map.137 = f32[3,128,256]{2,1,0:T(8,128)} custom-call(s32[3]{0:T(128)} %counts_ref.9, f32[8,256]{1,0:T(8,128)} %radial_ref.9, f32[256,128]{1,0:T(8,128)S(1)} %copy-done.1, f32[256,128]{1,0:T(8,128)S(1)} %copy-done, f32[3,128]{1,0:T(4,128)S(1)} %copy-done.4, bf16[32,192,128]{2,1,0:T(8,128)(2,1)S(1)} %all_to_all.21.got_ref, ...), custom_call_target="tpu_custom_call" | custom-call | flops 1409286144 | bytes 3145728 | tf_op jit(solution)/shard_map/pallas_call | solution.py:375
Async XLA Ops:
  0.6 0.7 copy-start.3
  8.4 11.0 %copy-start.10 = (bf16[256,128]{1,0:T(8,128)(2,1)S(1)}, bf16[256,128]{1,0:T(8,128)(2,1)}, u32[]{:S(2)}) copy-start(bf16[256,128]{1,0:T(8,128)(2,1)} %get-tuple-element.14) | copy-start | bytes 196612
  8.4 12.4 %copy-start.9 = (bf16[256,128]{1,0:T(8,128)(2,1)S(1)}, bf16[256,128]{1,0:T(8,128)(2,1)}, u32[]{:S(2)}) copy-start(bf16[256,128]{1,0:T(8,128)(2,1)} %get-tuple-element.15) | copy-start | bytes 196612
  8.4 13.7 %copy-start = (f32[256,128]{1,0:T(8,128)S(1)}, f32[256,128]{1,0:T(8,128)}, u32[]{:S(2)}) copy-start(f32[256,128]{1,0:T(8,128)} %constant.8.clone.damp_ref) | copy-start | bytes 393220
  8.4 13.7 %copy-start.1 = (f32[256,128]{1,0:T(8,128)S(1)}, f32[256,128]{1,0:T(8,128)}, u32[]{:S(2)}) copy-start(f32[256,128]{1,0:T(8,128)} %constant.7.clone.cent_ref) | copy-start | bytes 393220
  8.4 13.7 %copy-start.2 = (f32[256,256]{1,0:T(8,128)S(1)}, f32[256,256]{1,0:T(8,128)}, u32[]{:S(2)}) copy-start(f32[256,256]{1,0:T(8,128)} %constant.6.clone.kin_ref) | copy-start | bytes 786436
  8.4 13.7 %copy-start.4 = (f32[3,128]{1,0:T(4,128)S(1)}, f32[3,128]{1,0:T(4,128)}, u32[]{:S(2)}) copy-start(f32[3,128]{1,0:T(4,128)} %cor_ref.9) | copy-start | bytes 4612
  8.4 13.7 %copy-start.5 = (f32[3,128]{1,0:T(4,128)S(1)}, f32[3,128]{1,0:T(4,128)}, u32[]{:S(2)}) copy-start(f32[3,128]{1,0:T(4,128)} %e_ref.3) | copy-start | bytes 4612
  8.4 13.7 %copy-start.6 = (f32[3,128]{1,0:T(4,128)S(1)}, f32[3,128]{1,0:T(4,128)}, u32[]{:S(2)}) copy-start(f32[3,128]{1,0:T(4,128)} %rot_ref.3) | copy-start | bytes 4612
  8.5 34.6 %all-to-all-start = ((bf16[32,192,128]{2,1,0:T(8,128)(2,1)}), bf16[32,192,128]{2,1,0:T(8,128)(2,1)S(1)}, u32[]{:S(2)}, u32[]{:S(2)}) async-start(bf16[32,192,128]{2,1,0:T(8,128)(2,1)} %get-tuple-element.13), calls=%async_computation | async-start | bytes 3145728 | tf_op jit(solution)/shard_map/all_to_all | solution.py:266
  19.3 5.9 %collective-permute-start = (bf16[256,128]{1,0:T(8,128)(2,1)S(1)}, bf16[256,128]{1,0:T(8,128)(2,1)S(1)}, u32[]{:S(2)}, u32[]{:S(2)}) collective-permute-start(bf16[256,128]{1,0:T(8,128)(2,1)S(1)} %copy-done.10), channel_id=1, source_target_pairs={{0,1},{1,2},{2,3},{4,5},{5,6},{6,7},{8,9},{9,10},{10,11},{12,13},{... | collective-permute-start | bytes 196616 | tf_op jit(solution)/shard_map/ppermute | solution.py:262
  20.8 4.5 %collective-permute-start.1 = (bf16[256,128]{1,0:T(8,128)(2,1)S(1)}, bf16[256,128]{1,0:T(8,128)(2,1)S(1)}, u32[]{:S(2)}, u32[]{:S(2)}) collective-permute-start(bf16[256,128]{1,0:T(8,128)(2,1)S(1)} %copy-done.9), channel_id=1, source_target_pairs={{1,0},{2,1},{3,2},{5,4},{6,5},{7,6},{9,8},{10,9},{11,10},{13,12},{... | collective-permute-start | bytes 196616 | tf_op jit(solution)/shard_map/ppermute | solution.py:262
  82.0 5.0 %copy-start.8 = (bf16[256,128]{1,0:T(8,128)(2,1)S(1)}, bf16[256,128]{1,0:T(8,128)(2,1)}, u32[]{:S(2)}) copy-start(bf16[256,128]{1,0:T(8,128)(2,1)} %get-tuple-element.20) | copy-start | bytes 196612
  82.0 6.9 %copy-start.7 = (bf16[256,128]{1,0:T(8,128)(2,1)S(1)}, bf16[256,128]{1,0:T(8,128)(2,1)}, u32[]{:S(2)}) copy-start(bf16[256,128]{1,0:T(8,128)(2,1)} %get-tuple-element.21) | copy-start | bytes 196612
  82.0 29.2 %all-to-all-start.2 = ((bf16[32,192,128]{2,1,0:T(8,128)(2,1)}), bf16[32,192,128]{2,1,0:T(8,128)(2,1)S(1)}, u32[]{:S(2)}, u32[]{:S(2)}) async-start(bf16[32,192,128]{2,1,0:T(8,128)(2,1)} %get-tuple-element.18), calls=%async_computation.2 | async-start | bytes 3145728 | tf_op jit(solution)/shard_map/all_to_all | solution.py:266
  87.0 7.1 %collective-permute-start.2 = (bf16[256,128]{1,0:T(8,128)(2,1)S(1)}, bf16[256,128]{1,0:T(8,128)(2,1)S(1)}, u32[]{:S(2)}, u32[]{:S(2)}) collective-permute-start(bf16[256,128]{1,0:T(8,128)(2,1)S(1)} %copy-done.8), channel_id=1, source_target_pairs={{0,1},{1,2},{2,3},{4,5},{5,6},{6,7},{8,9},{9,10},{10,11},{12,13},{... | collective-permute-start | bytes 196616 | tf_op jit(solution)/shard_map/ppermute | solution.py:262
  88.9 5.2 %collective-permute-start.3 = (bf16[256,128]{1,0:T(8,128)(2,1)S(1)}, bf16[256,128]{1,0:T(8,128)(2,1)S(1)}, u32[]{:S(2)}, u32[]{:S(2)}) collective-permute-start(bf16[256,128]{1,0:T(8,128)(2,1)S(1)} %copy-done.7), channel_id=1, source_target_pairs={{1,0},{2,1},{3,2},{5,4},{6,5},{7,6},{9,8},{10,9},{11,10},{13,12},{... | collective-permute-start | bytes 196616 | tf_op jit(solution)/shard_map/ppermute | solution.py:262

commit v3 on v2

--- a/solution.py
+++ b/solution.py
@@ -47,13 +47,14 @@
     return (channel < counts_ref[h]).astype(F32)
 
 
-def radial_columns(radial_ref, shape):
+def radial_columns(radial_ref, columns_ref):
     columns = radial_ref[...].T
-    return [jnp.broadcast_to(columns[:, l : l + 1], shape) for l in range(columns.shape[1])]
+    for l in range(columns.shape[1]):
+        columns_ref[l] = jnp.broadcast_to(columns[:, l : l + 1], columns_ref.shape[1:])
 
 
 def weight(wide, columns):
-    return jnp.concatenate([(wide * column).astype(BF) for column in columns], axis=1)
+    return jnp.concatenate([(wide * columns[l]).astype(BF) for l in range(columns.shape[0])], axis=1)
 
 
 def interleave(a, b, count):
@@ -66,7 +67,7 @@
     count, rows = send_ref.shape[:2]
     pair = rows // 4
     wide = field.astype(BF).astype(F32)
-    weighted = jnp.concatenate([(wide * column).astype(BF) for column in columns], axis=1)
+    weighted = jnp.concatenate([(wide * columns[l]).astype(BF) for l in range(columns.shape[0])], axis=1)
     if arrived is not None:
         arrived()
     send_ref[:, :pair, :] = interleave(wide, dot_nn(weighted, blocks_ref[0].reshape(-1, width)), count)
@@ -93,12 +94,20 @@
     return [functools.partial(arrive, h) for h in range(len(copies))]
 
 
-def emit_edges(h, field, cor_ref, up_ref, down_ref):
+def odd_group():
+    return lax.rem(lax.axis_index("hel"), 2) == 1
+
+
+def emit_edges(fields_ref, cor_ref, edge_ref, inner_ref, outer_ref, sem):
     last = cor_ref.shape[0] - 1
-    if h == last:
-        up_ref[...] = (field * cor_ref[last : last + 1, :]).astype(BF)
-    if h == 0:
-        down_ref[...] = field.astype(BF)
+    up = (fields_ref[last] * cor_ref[last : last + 1, :]).astype(BF)
+    down = fields_ref[0].astype(BF)
+    edge_ref[0] = jnp.where(odd_group(), down, up)
+    edge_ref[1] = jnp.where(odd_group(), up, down)
+    copies = [pltpu.make_async_copy(edge_ref.at[k], ref, sem.at[k]) for k, ref in enumerate((inner_ref, outer_ref))]
+    for copy in copies:
+        copy.start()
+    return copies
 
 
 def copy_out(h, made_ref, send_ref, sem):
@@ -109,24 +118,29 @@
 
 
 def first_kernel(
-    counts_ref, radial_ref, cor_ref, psi_ref, blocks_ref, field_ref, up_ref, down_ref, send_ref,
-    here_ref, kept_ref, made_ref, psi_sem, block_sem, send_sem,
+    counts_ref, radial_hbm, cor_hbm, psi_ref, blocks_ref, field_ref, inner_ref, outer_ref, send_ref,
+    here_ref, radial_ref, cor_ref, columns_ref, kept_ref, made_ref, edge_ref, small_sem, psi_sem, block_sem, edge_sem, send_sem,
 ):
     helicities, _, width = field_ref.shape
     psi = [pltpu.make_async_copy(psi_ref.at[h], here_ref.at[h], psi_sem.at[h]) for h in range(helicities)]
-    psi[0].start()
+    small = [
+        pltpu.make_async_copy(radial_hbm, radial_ref, small_sem.at[0]),
+        pltpu.make_async_copy(cor_hbm, cor_ref, small_sem.at[1]),
+    ]
+    for copy in small + psi:
+        copy.start()
     arrived = fetch(blocks_ref, kept_ref, block_sem)
-    for copy in psi[1:]:
-        copy.start()
-    columns = radial_columns(radial_ref, field_ref.shape[1:])
+    for copy in small:
+        copy.wait()
+    radial_columns(radial_ref, columns_ref)
     sent = []
     for h in range(helicities):
         psi[h].wait()
         field = here_ref[h].T * active_row(counts_ref, h, width)
         field_ref[h] = field
-        emit_edges(h, field, cor_ref, up_ref, down_ref)
-        emit_products(field, kept_ref.at[h], columns, made_ref.at[h], arrived[h])
+        emit_products(field, kept_ref.at[h], columns_ref, made_ref.at[h], arrived[h])
         sent.append(copy_out(h, made_ref, send_ref, send_sem))
+    sent += emit_edges(field_ref, cor_ref, edge_ref, inner_ref, outer_ref, edge_sem)
     for copy in sent:
         copy.wait()
 
@@ -179,7 +193,8 @@
     terms = blocks_ref.shape[3]
     cent = cent_ref[...]
     damp = damp_ref[...]
-    columns = radial_columns(radial_ref, (points, width))
+    columns = refs[-1]
+    radial_columns(radial_ref, columns)
     for h in range(helicities):
         mask = active_row(counts_ref, h, width)
         field = field_ref[h]
@@ -201,7 +216,7 @@
             refs[0][h] = field.T
 
 
-def renew(h, got_ref, counts_ref, local_ref, columns, cent_ref, damp_ref, cor_ref, below_ref, above_ref, kept_ref, arrived):
+def renew(h, got_ref, counts_ref, local_ref, columns, cent_ref, damp_ref, cor_ref, inner_ref, outer_ref, kept_ref, arrived):
     helicities, points, width = local_ref.shape
     rows = got_ref.shape[1] // helicities
     pair = rows // 4
@@ -211,43 +226,45 @@
         slots += [both[:, : pair // 2].reshape(points, width), both[:, pair // 2 :].reshape(points, width)]
     total = slots[-1]
     if h == 0:
-        total = total - cent_ref[...] * below_ref[...].astype(F32)
+        below = jnp.where(odd_group(), inner_ref[...], outer_ref[...])
+        total = total - cent_ref[...] * below.astype(F32)
     if h == helicities - 1:
-        total = total - cent_ref[...] * (above_ref[...].astype(F32) * cor_ref[h : h + 1, :])
+        above = jnp.where(odd_group(), outer_ref[...], inner_ref[...])
+        total = total - cent_ref[...] * (above.astype(F32) * cor_ref[h : h + 1, :])
     sources = [slot.astype(BF) for slot in slots[:-1]]
     total = forward(sources, [kept_ref.at[h, j] for j in range(SIDES)], columns, total, arrived[h])
     return local_ref[h] + 2.0 * damp_ref[...] * (active_row(counts_ref, h, width) * total)
 
 
 def middle_kernel(
-    counts_ref, radial_ref, cent_ref, damp_ref, cor_ref, got_ref, local_ref, below_ref, above_ref, blocks_ref,
-    field_ref, up_ref, down_ref, send_ref, kept_ref, made_ref, block_sem, send_sem,
+    counts_ref, radial_ref, cent_ref, damp_ref, cor_ref, got_ref, local_ref, inner_got, outer_got, blocks_ref,
+    field_ref, inner_ref, outer_ref, send_ref, columns, kept_ref, made_ref, edge_ref, block_sem, edge_sem, send_sem,
 ):
     arrived = fetch(blocks_ref, kept_ref, block_sem)
-    columns = radial_columns(radial_ref, local_ref.shape[1:])
+    radial_columns(radial_ref, columns)
     sent = []
     for h in range(local_ref.shape[0]):
         field = renew(
-            h, got_ref, counts_ref, local_ref, columns, cent_ref, damp_ref, cor_ref, below_ref, above_ref, kept_ref, arrived
+            h, got_ref, counts_ref, local_ref, columns, cent_ref, damp_ref, cor_ref, inner_got, outer_got, kept_ref, arrived
         )
         field_ref[h] = field
-        emit_edges(h, field, cor_ref, up_ref, down_ref)
         emit_products(field, kept_ref.at[h], columns, made_ref.at[h])
         sent.append(copy_out(h, made_ref, send_ref, send_sem))
+    sent += emit_edges(field_ref, cor_ref, edge_ref, inner_ref, outer_ref, edge_sem)
     for copy in sent:
         copy.wait()
 
 
 def last_kernel(
-    counts_ref, radial_ref, cent_ref, damp_ref, cor_ref, got_ref, local_ref, below_ref, above_ref, blocks_ref, out_ref,
-    kept_ref, made_ref, block_sem, sem,
+    counts_ref, radial_ref, cent_ref, damp_ref, cor_ref, got_ref, local_ref, inner_got, outer_got, blocks_ref, out_ref,
+    columns, kept_ref, made_ref, block_sem, sem,
 ):
     arrived = fetch(blocks_ref, kept_ref, block_sem)
-    columns = radial_columns(radial_ref, local_ref.shape[1:])
+    radial_columns(radial_ref, columns)
     sent = []
     for h in range(local_ref.shape[0]):
         field = renew(
-            h, got_ref, counts_ref, local_ref, columns, cent_ref, damp_ref, cor_ref, below_ref, above_ref, kept_ref, arrived
+            h, got_ref, counts_ref, local_ref, columns, cent_ref, damp_ref, cor_ref, inner_got, outer_got, kept_ref, arrived
         )
         made_ref[h] = field.T
         copy = pltpu.make_async_copy(made_ref.at[h], out_ref.at[h], sem.at[h])
@@ -257,9 +274,10 @@
         copy.wait()
 
 
-def shifted(x, axis, by):
+def swapped(x, axis, first):
     peers = lax.axis_size(axis)
-    return lax.ppermute(x, axis, [(i, i + by) for i in range(peers) if 0 <= i + by < peers])
+    pairs = [(i, i + 1) for i in range(first, peers - 1, 2)]
+    return lax.ppermute(x, axis, pairs + [(j, i) for i, j in pairs])
 
 
 def exchange(x):
@@ -280,16 +298,16 @@
     hbm = pl.BlockSpec(memory_space=pl.ANY)
     whole = lambda a: pl.BlockSpec(a.shape, lambda *_: (0,) * a.ndim)
     place = lambda a: pltpu.with_memory_space_constraint(a, pltpu.HBM)
-    psi_cur, psi_prev, blocks, radial_terms, counts, offsets = map(
-        place, (psi_cur, psi_prev, blocks, radial_terms, counts, offsets)
-    )
+    psi_cur, psi_prev, blocks, counts, offsets = map(place, (psi_cur, psi_prev, blocks, counts, offsets))
 
     field_shape = (helicities, points, width)
     field_out = pltpu.VMEM(field_shape, F32)
     parcel_shape = (count, helicities * rows, width)
     parcel_out = pltpu.HBM(parcel_shape, BF)
     edge_out = pltpu.HBM((points, width), BF)
-    edge = pl.BlockSpec(edge_out.shape, lambda *_: (0, 0))
+    edges = pltpu.VMEM((2, points, width), BF)
+    pair = pltpu.SemaphoreType.DMA((2,))
+    columns = pltpu.VMEM((terms, points, width), F32)
     made = pltpu.VMEM((helicities, count, rows, width), BF)
     kept = pltpu.VMEM((helicities, SIDES) + blocks.shape[3:], BF)
     copies = pltpu.SemaphoreType.DMA((helicities,))
@@ -311,12 +329,15 @@
 
     first = call(
         first_kernel,
-        [smem, whole(radial_terms), whole(coriolis), hbm, hbm],
-        [vmem, edge, edge, hbm],
+        [smem, hbm, hbm, hbm, hbm],
+        [vmem, hbm, hbm, hbm],
         [field_out, edge_out, edge_out, parcel_out],
         SIDES * mac,
         blocks.size * 2,
-        [pltpu.VMEM(psi_cur.shape, F32), kept, made, copies, parts, copies],
+        [
+            pltpu.VMEM(psi_cur.shape, F32), pltpu.VMEM(radial_terms.shape, F32), pltpu.VMEM(coriolis.shape, F32), columns, kept,
+            made, edges, pair, copies, parts, pair, copies,
+        ],
     )
     route = call(
         route_kernel,
@@ -335,17 +356,17 @@
             tables[0] = vmem
         out_specs = [vmem, whole(psi_prev)] if final else vmem
         out_shape = [field_out, pltpu.HBM(psi_prev.shape, F32)] if final else field_out
-        return call(kernel, [smem] + tables + [vmem, diagonal], out_specs, out_shape, 2 * mac, 4 * psi_cur.size)
-
-    given = [smem, *[whole(a) for a in (radial_terms, cent, damp, coriolis)], vmem, vmem, edge, edge, hbm]
+        return call(kernel, [smem] + tables + [vmem, diagonal], out_specs, out_shape, 2 * mac, 4 * psi_cur.size, [columns])
+
+    given = [smem] + [vmem] * 8 + [hbm]
     middle = call(
         middle_kernel,
         given,
-        [vmem, edge, edge, hbm],
+        [vmem, hbm, hbm, hbm],
         [field_out, edge_out, edge_out, parcel_out],
         2 * SIDES * mac,
         blocks.size,
-        [kept, made, parts, copies],
+        [columns, kept, made, edges, parts, pair, copies],
     )
     final = call(
         last_kernel,
@@ -354,27 +375,27 @@
         pltpu.HBM(psi_cur.shape, F32),
         SIDES * mac,
         blocks.size,
-        [kept, pltpu.VMEM(psi_cur.shape, F32), parts, copies],
+        [columns, kept, pltpu.VMEM(psi_cur.shape, F32), parts, copies],
     )
 
-    field, up, down, send = first(counts, radial_terms, coriolis, psi_cur, blocks)
+    field, inner, outer, send = first(counts, place(radial_terms), place(coriolis), psi_cur, blocks)
     prev = psi_prev
     for iteration in range(STEPS):
         ends = iteration + 1 == STEPS
         got = exchange(send)
-        below = shifted(up, "hel", 1)
-        above = shifted(down, "hel", -1)
+        outer = swapped(outer, "hel", 1)
+        inner = swapped(inner, "hel", 0)
         rest = local(iteration > 0)(
             counts, prev, radial_terms, kinetic, cent, damp, energies, rotation, coriolis, field, blocks
         )
         if ends:
             rest, before = rest
-        back = exchange(route(offsets, got, rest, below, above))
-        given = (counts, radial_terms, cent, damp, coriolis, back, rest, below, above, blocks)
+        back = exchange(route(offsets, got, rest, inner, outer))
+        given = (counts, radial_terms, cent, damp, coriolis, back, rest, inner, outer, blocks)
         if ends:
             return before, final(*given)
         prev = field
-        field, up, down, send = middle(*given)
+        field, inner, outer, send = middle(*given)
 
 
 def solution(mesh):

time: 147 us -> 146 us (level)
  starting transfers between devices: 21.9 us -> 17.4 us
  waiting for transfers between devices: 34.9 us -> 39.2 us
    ppermute x4, starting transfers between devices: 6.08 us -> 1.68 us  [swapped(): return lax.ppermute(x, axis, pairs + [(j, i) for i, j in pairs])]
    all_to_all x2, waiting for transfers between devices: 34.9 us -> 39.2 us  [exchange(): return lax.all_to_all(x, 'chan', 0, 0, tiled=True)]
where the time goes in v3:
time: 146 us
  blocking collectives  57.6 us (39%)
  waiting for transfers between devices  39.2 us (27%)
  Pallas kernels  30.3 us (21%)
  starting transfers between devices  17.4 us (12%)
    all_to_all x2, blocking collectives, exchange(): return lax.all_to_all(x, 'chan', 0, 0, tiled=True)  57.6 us
    all_to_all x2, waiting for transfers between devices, exchange(): return lax.all_to_all(x, 'chan', 0, 0, tiled=True)  39.2 us
    all_to_all x2, starting transfers between devices, exchange(): return lax.all_to_all(x, 'chan', 0, 0, tiled=True)  15.7 us
    pallas_call x1, Pallas kernels, body(): field, inner, outer, send = middle(*given)  7.68 us
    pallas_call x1, Pallas kernels, body(): first(counts, place(radial_terms), place(coriolis), psi_cur, blocks)  7.13 us
    pallas_call x2, Pallas kernels, body(): local(iteration > 0)  6.78 us
    pallas_call x1, Pallas kernels, body(): return (before, final(*given))  5.49 us
    pallas_call x2, Pallas kernels, body(): back = exchange(route(offsets, got, rest, inner, outer))  3.2 us
  transfers between devices with their start and end apart: 6, of which 2 were waited for; matrix products, arithmetic and copies ran while one was open for 0% of the time, Pallas kernels for 5%

profile of v3, /device:TPU:0, one launch (start us, length us, event | category | flops | bytes accessed | tf_op | source)
XLA Modules:
  0.0 145.6 jit_solution(13086210907736595449)
XLA Ops:
  0.6 7.1 %shard_map.131 = (f32[3,256,128]{2,1,0:T(8,128)S(1)}, bf16[256,128]{1,0:T(8,128)(2,1)}, bf16[256,128]{1,0:T(8,128)(2,1)}, bf16[32,192,128]{2,1,0:T(8,128)(2,1)}) custom-call(s32[3]{0:T(128)} %counts_ref.9, f32[8,256]{1,0:T(8,128)} %radial_ref.7, f32[3,128]{1,0:T(4,128)} %cor_ref.7, f32[3,128,256]{2,1,0:T(8,128)} %psi_ref.1, ...), custom_call_target="tpu_custom_call" | custom-call | flops 1409286144 | bytes 6291456 | tf_op jit(solution)/shard_map/pallas_call | solution.py:381
  7.8 0.0 copy-start.9
  7.8 0.0 copy-start.8
  7.8 0.0 copy-start
  7.8 0.0 copy-start.1
  7.8 0.0 copy-start.2
  7.8 0.0 copy-start.3
  7.8 0.0 copy-start.4
  7.8 0.0 copy-start.5
  7.9 0.0 copy-start.6
  7.9 10.9 %all-to-all-start = ((bf16[32,192,128]{2,1,0:T(8,128)(2,1)}), bf16[32,192,128]{2,1,0:T(8,128)(2,1)S(1)}, u32[]{:S(2)}, u32[]{:S(2)}) async-start(bf16[32,192,128]{2,1,0:T(8,128)(2,1)} %get-tuple-element.13), calls=%async_computation | async-start | bytes 3145728 | tf_op jit(solution)/shard_map/all_to_all | solution.py:284
  18.7 0.0 copy-done.9
  18.8 0.1 collective-permute-start
  18.8 0.0 copy-done.8
  18.9 0.7 collective-permute-start.1
  19.5 0.0 copy-done
  19.5 0.0 copy-done.1
  19.5 0.0 copy-done.2
  19.6 0.0 copy-done.3
  19.6 0.0 copy-done.4
  19.6 0.0 copy-done.5
  19.6 0.0 copy-done.6
  19.6 3.1 %shard_map.132.refs_0_.local_ref = f32[3,256,128]{2,1,0:T(8,128)S(1)} custom-call(s32[3]{0:T(128)} %counts_ref.9, f32[3,128,256]{2,1,0:T(8,128)} %prev_ref.1, f32[8,256]{1,0:T(8,128)S(1)} %copy-done.3, f32[256,256]{1,0:T(8,128)S(1)} %copy-done.2, f32[256,128]{1,0:T(8,128)S(1)} %copy-done.1, f32[256,128]{1,0:T(8,128)S(1)} %copy-done, f32[3,128]{1,0:T(4,128)S(1)} %copy-done.5, ...), custom_call_target="tpu_custom_call" | custom-call | flops 402653184 | bytes 393216 | tf_op jit(solution)/shard_map/pallas_call | solution.py:388
  22.7 0.0 collective-permute-done.refs_1_.inner_got
  22.7 0.0 collective-permute-done.1.refs_2_.outer_got
  22.7 19.8 %all-to-all-done.got_ref = bf16[32,192,128]{2,1,0:T(8,128)(2,1)S(1)} async-done(((bf16[32,192,128]{2,1,0:T(8,128)(2,1)}), bf16[32,192,128]{2,1,0:T(8,128)(2,1)S(1)}, u32[]{:S(2)}, u32[]{:S(2)}) %all-to-all-start) | async-done | bytes 1572896 | tf_op jit(solution)/shard_map/all_to_all | solution.py:284
  42.5 1.6 %shard_map.133 = bf16[32,192,128]{2,1,0:T(8,128)(2,1)S(1)} custom-call(s32[3,7]{1,0:T(4,128)} %offsets_ref.3, bf16[32,192,128]{2,1,0:T(8,128)(2,1)S(1)} %all-to-all-done.got_ref, f32[3,256,128]{2,1,0:T(8,128)S(1)} %shard_map.132.refs_0_.local_ref, bf16[256,128]{1,0:T(8,128)(2,1)S(1)} %collective-permute-done.refs_1_.inner_got, ...), custom_call_target="tpu_custom_call" | custom-call | flops 786432 | bytes 393216 | tf_op jit(solution)/shard_map/pallas_call | solution.py:393
  44.1 29.4 %all_to_all.20.got_ref = bf16[32,192,128]{2,1,0:T(8,128)(2,1)S(1)} all-to-all(bf16[32,192,128]{2,1,0:T(8,128)(2,1)S(1)} %shard_map.133), channel_id=1, replica_groups=mesh['chan'=32,'hel'=4] {'chan'}, dimensions={0} | all-to-all | bytes 3145728 | tf_op jit(solution)/shard_map/all_to_all | solution.py:284
  73.5 7.7 %shard_map.134 = (f32[3,256,128]{2,1,0:T(8,128)S(1)}, bf16[256,128]{1,0:T(8,128)(2,1)}, bf16[256,128]{1,0:T(8,128)(2,1)}, bf16[32,192,128]{2,1,0:T(8,128)(2,1)}) custom-call(s32[3]{0:T(128)} %counts_ref.9, f32[8,256]{1,0:T(8,128)S(1)} %copy-done.3, f32[256,128]{1,0:T(8,128)S(1)} %copy-done.1, f32[256,128]{1,0:T(8,128)S(1)} %copy-done, ...), custom_call_target="tpu_custom_call" | custom-call | flops 2818572288 | bytes 3145728 | tf_op jit(solution)/shard_map/pallas_call | solution.py:398
  81.2 0.0 copy-start.7
  81.2 4.8 %all-to-all-start.2 = ((bf16[32,192,128]{2,1,0:T(8,128)(2,1)}), bf16[32,192,128]{2,1,0:T(8,128)(2,1)S(1)}, u32[]{:S(2)}, u32[]{:S(2)}) async-start(bf16[32,192,128]{2,1,0:T(8,128)(2,1)} %get-tuple-element.18), calls=%async_computation.2 | async-start | bytes 3145728 | tf_op jit(solution)/shard_map/all_to_all | solution.py:284
  86.0 0.1 collective-permute-start.2
  86.1 0.0 copy-done.7
  86.1 0.8 collective-permute-start.3
  87.0 3.7 %shard_map.135 = (f32[3,256,128]{2,1,0:T(8,128)S(1)}, f32[3,128,256]{2,1,0:T(8,128)}) custom-call(s32[3]{0:T(128)} %counts_ref.9, f32[3,256,128]{2,1,0:T(8,128)S(1)} %get-tuple-element.12.field_ref.prev_ref, f32[8,256]{1,0:T(8,128)S(1)} %copy-done.3, f32[256,256]{1,0:T(8,128)S(1)} %copy-done.2, f32[256,128]{1,0:T(8,128)S(1)} %copy-done.1, ...), custom_call_target="tpu_custom_call" | custom-call | flops 402653184 | bytes 393216 | tf_op jit(solution)/shard_map/pallas_call | solution.py:388
  90.7 0.0 collective-permute-done.2.refs_1_.inner_got
  90.7 0.0 collective-permute-done.3.refs_2_.outer_got
  90.7 19.4 %all-to-all-done.2.got_ref = bf16[32,192,128]{2,1,0:T(8,128)(2,1)S(1)} async-done(((bf16[32,192,128]{2,1,0:T(8,128)(2,1)}), bf16[32,192,128]{2,1,0:T(8,128)(2,1)S(1)}, u32[]{:S(2)}, u32[]{:S(2)}) %all-to-all-start.2) | async-done | bytes 1572896 | tf_op jit(solution)/shard_map/all_to_all | solution.py:284
  110.1 1.6 %shard_map.136 = bf16[32,192,128]{2,1,0:T(8,128)(2,1)S(1)} custom-call(s32[3,7]{1,0:T(4,128)} %offsets_ref.3, bf16[32,192,128]{2,1,0:T(8,128)(2,1)S(1)} %all-to-all-done.2.got_ref, f32[3,256,128]{2,1,0:T(8,128)S(1)} %get-tuple-element.19.refs_0_.local_ref, bf16[256,128]{1,0:T(8,128)(2,1)S(1)} %collective-permute-done.2.refs_1_.inner_got, ...), custom_call_target="tpu_custom_call" | custom-call | flops 786432 | bytes 393216 | tf_op jit(solution)/shard_map/pallas_call | solution.py:393
  111.7 28.2 %all_to_all.21.got_ref = bf16[32,192,128]{2,1,0:T(8,128)(2,1)S(1)} all-to-all(bf16[32,192,128]{2,1,0:T(8,128)(2,1)S(1)} %shard_map.136), channel_id=1, replica_groups=mesh['chan'=32,'hel'=4] {'chan'}, dimensions={0} | all-to-all | bytes 3145728 | tf_op jit(solution)/shard_map/all_to_all | solution.py:284
  139.9 5.5 %shard_map.137 = f32[3,128,256]{2,1,0:T(8,128)} custom-call(s32[3]{0:T(128)} %counts_ref.9, f32[8,256]{1,0:T(8,128)S(1)} %copy-done.3, f32[256,128]{1,0:T(8,128)S(1)} %copy-done.1, f32[256,128]{1,0:T(8,128)S(1)} %copy-done, f32[3,128]{1,0:T(4,128)S(1)} %copy-done.4, bf16[32,192,128]{2,1,0:T(8,128)(2,1)S(1)} %all_to_all.21.got_ref, ...), custom_call_target="tpu_custom_call" | custom-call | flops 1409286144 | bytes 3145728 | tf_op jit(solution)/shard_map/pallas_call | solution.py:396
Async XLA Ops:
  7.8 11.0 %copy-start.9 = (bf16[256,128]{1,0:T(8,128)(2,1)S(1)}, bf16[256,128]{1,0:T(8,128)(2,1)}, u32[]{:S(2)}) copy-start(bf16[256,128]{1,0:T(8,128)(2,1)} %get-tuple-element.14) | copy-start | bytes 196612
  7.8 11.1 %copy-start.8 = (bf16[256,128]{1,0:T(8,128)(2,1)S(1)}, bf16[256,128]{1,0:T(8,128)(2,1)}, u32[]{:S(2)}) copy-start(bf16[256,128]{1,0:T(8,128)(2,1)} %get-tuple-element.15) | copy-start | bytes 196612
  7.8 11.7 %copy-start = (f32[256,128]{1,0:T(8,128)S(1)}, f32[256,128]{1,0:T(8,128)}, u32[]{:S(2)}) copy-start(f32[256,128]{1,0:T(8,128)} %constant.8.clone.damp_ref) | copy-start | bytes 393220
  7.8 11.7 %copy-start.1 = (f32[256,128]{1,0:T(8,128)S(1)}, f32[256,128]{1,0:T(8,128)}, u32[]{:S(2)}) copy-start(f32[256,128]{1,0:T(8,128)} %constant.7.clone.cent_ref) | copy-start | bytes 393220
  7.8 11.7 %copy-start.2 = (f32[256,256]{1,0:T(8,128)S(1)}, f32[256,256]{1,0:T(8,128)}, u32[]{:S(2)}) copy-start(f32[256,256]{1,0:T(8,128)} %constant.6.clone.kin_ref) | copy-start | bytes 786436
  7.8 11.7 %copy-start.3 = (f32[8,256]{1,0:T(8,128)S(1)}, f32[8,256]{1,0:T(8,128)}, u32[]{:S(2)}) copy-start(f32[8,256]{1,0:T(8,128)} %radial_ref.7) | copy-start | bytes 24580
  7.8 11.7 %copy-start.4 = (f32[3,128]{1,0:T(4,128)S(1)}, f32[3,128]{1,0:T(4,128)}, u32[]{:S(2)}) copy-start(f32[3,128]{1,0:T(4,128)} %cor_ref.7) | copy-start | bytes 4612
  7.8 11.7 %copy-start.5 = (f32[3,128]{1,0:T(4,128)S(1)}, f32[3,128]{1,0:T(4,128)}, u32[]{:S(2)}) copy-start(f32[3,128]{1,0:T(4,128)} %e_ref.3) | copy-start | bytes 4612
  7.9 11.7 %copy-start.6 = (f32[3,128]{1,0:T(4,128)S(1)}, f32[3,128]{1,0:T(4,128)}, u32[]{:S(2)}) copy-start(f32[3,128]{1,0:T(4,128)} %rot_ref.3) | copy-start | bytes 4612
  7.9 34.6 %all-to-all-start = ((bf16[32,192,128]{2,1,0:T(8,128)(2,1)}), bf16[32,192,128]{2,1,0:T(8,128)(2,1)S(1)}, u32[]{:S(2)}, u32[]{:S(2)}) async-start(bf16[32,192,128]{2,1,0:T(8,128)(2,1)} %get-tuple-element.13), calls=%async_computation | async-start | bytes 3145728 | tf_op jit(solution)/shard_map/all_to_all | solution.py:284
  18.8 3.9 %collective-permute-start = (bf16[256,128]{1,0:T(8,128)(2,1)S(1)}, bf16[256,128]{1,0:T(8,128)(2,1)S(1)}, u32[]{:S(2)}, u32[]{:S(2)}) collective-permute-start(bf16[256,128]{1,0:T(8,128)(2,1)S(1)} %copy-done.9), channel_id=1, source_target_pairs={{0,1},{2,3},{1,0},{3,2},{4,5},{6,7},{5,4},{7,6},{8,9},{10,11},{9,8... | collective-permute-start | bytes 196616 | tf_op jit(solution)/shard_map/ppermute | solution.py:280
  18.9 3.8 %collective-permute-start.1 = (bf16[256,128]{1,0:T(8,128)(2,1)S(1)}, bf16[256,128]{1,0:T(8,128)(2,1)S(1)}, u32[]{:S(2)}, u32[]{:S(2)}) collective-permute-start(bf16[256,128]{1,0:T(8,128)(2,1)S(1)} %copy-done.8), channel_id=1, source_target_pairs={{1,2},{2,1},{5,6},{6,5},{9,10},{10,9},{13,14},{14,13},{17,18},{18,... | collective-permute-start | bytes 196616 | tf_op jit(solution)/shard_map/ppermute | solution.py:280
  81.2 5.0 %copy-start.7 = (bf16[256,128]{1,0:T(8,128)(2,1)S(1)}, bf16[256,128]{1,0:T(8,128)(2,1)}, u32[]{:S(2)}) copy-start(bf16[256,128]{1,0:T(8,128)(2,1)} %get-tuple-element.21) | copy-start | bytes 196612
  81.2 28.9 %all-to-all-start.2 = ((bf16[32,192,128]{2,1,0:T(8,128)(2,1)}), bf16[32,192,128]{2,1,0:T(8,128)(2,1)S(1)}, u32[]{:S(2)}, u32[]{:S(2)}) async-start(bf16[32,192,128]{2,1,0:T(8,128)(2,1)} %get-tuple-element.18), calls=%async_computation.2 | async-start | bytes 3145728 | tf_op jit(solution)/shard_map/all_to_all | solution.py:284
  86.0 4.7 %collective-permute-start.2 = (bf16[256,128]{1,0:T(8,128)(2,1)}, bf16[256,128]{1,0:T(8,128)(2,1)S(1)}, u32[]{:S(2)}, u32[]{:S(2)}) collective-permute-start(bf16[256,128]{1,0:T(8,128)(2,1)} %get-tuple-element.20), channel_id=1, source_target_pairs={{0,1},{2,3},{1,0},{3,2},{4,5},{6,7},{5,4},{7,6},{8,9},{10,11},{9,8... | collective-permute-start | bytes 196616 | tf_op jit(solution)/shard_map/ppermute | solution.py:280
  86.1 4.6 %collective-permute-start.3 = (bf16[256,128]{1,0:T(8,128)(2,1)S(1)}, bf16[256,128]{1,0:T(8,128)(2,1)S(1)}, u32[]{:S(2)}, u32[]{:S(2)}) collective-permute-start(bf16[256,128]{1,0:T(8,128)(2,1)S(1)} %copy-done.7), channel_id=1, source_target_pairs={{1,2},{2,1},{5,6},{6,5},{9,10},{10,9},{13,14},{14,13},{17,18},{18,... | collective-permute-start | bytes 196616 | tf_op jit(solution)/shard_map/ppermute | solution.py:280

commit v4 on v3

--- a/solution.py
+++ b/solution.py
@@ -12,6 +12,7 @@
 BF = jnp.bfloat16
 F32 = jnp.float32
 VMEM_LIMIT = 24 * 1024 * 1024
+AHEAD = 3
 SIDES = 7
 
 
@@ -77,21 +78,13 @@
         send_ref[:, p * pair : (p + 1) * pair, :] = interleave(out[:, :width], out[:, width:], count)
 
 
-def fetch(blocks_ref, kept_ref, sem):
-    copies = []
-    for h in range(blocks_ref.shape[0]):
-        copies.append([])
-        for k, at in enumerate(range(0, SIDES, 2)):
-            size = min(2, SIDES - at)
-            source = blocks_ref.at[h, 0, pl.ds(1 + at, size)]
-            copies[h].append(pltpu.make_async_copy(source, kept_ref.at[h, pl.ds(at, size)], sem.at[h, k]))
-            copies[h][-1].start()
-
-    def arrive(h):
-        for copy in copies[h]:
-            copy.wait()
-
-    return [functools.partial(arrive, h) for h in range(len(copies))]
+def fetch(blocks_ref, kept_ref, sem, skip=0):
+    arrived = [None] * skip
+    for h in range(skip, blocks_ref.shape[0]):
+        copy = pltpu.make_async_copy(blocks_ref.at[h, 0, pl.ds(1, SIDES)], kept_ref.at[h], sem.at[h])
+        copy.start()
+        arrived.append(copy.wait)
+    return arrived
 
 
 def odd_group():
@@ -138,9 +131,10 @@
         psi[h].wait()
         field = here_ref[h].T * active_row(counts_ref, h, width)
         field_ref[h] = field
+        if h + 1 == field_ref.shape[0]:
+            sent += emit_edges(field_ref, cor_ref, edge_ref, inner_ref, outer_ref, edge_sem)
         emit_products(field, kept_ref.at[h], columns_ref, made_ref.at[h], arrived[h])
         sent.append(copy_out(h, made_ref, send_ref, send_sem))
-    sent += emit_edges(field_ref, cor_ref, edge_ref, inner_ref, outer_ref, edge_sem)
     for copy in sent:
         copy.wait()
 
@@ -187,13 +181,18 @@
 
 
 def local_kernel(
-    final, counts_ref, prev_ref, radial_ref, kin_ref, cent_ref, damp_ref, e_ref, rot_ref, cor_ref, field_ref, blocks_ref, out_ref, *refs
+    final, counts_ref, prev_ref, radial_ref, kin_ref, cent_ref, damp_ref, e_ref, rot_ref, cor_ref, field_ref, blocks_ref, all_blocks_ref, out_ref, columns, *refs
 ):
     helicities, points, width = field_ref.shape
     terms = blocks_ref.shape[3]
     cent = cent_ref[...]
     damp = damp_ref[...]
-    columns = refs[-1]
+    ahead_sem = refs[-1]
+    ahead = [
+        pltpu.make_async_copy(all_blocks_ref.at[h, 0, pl.ds(1, SIDES)], refs[h], ahead_sem.at[h]) for h in range(AHEAD)
+    ]
+    for copy in ahead:
+        copy.start()
     radial_columns(radial_ref, columns)
     for h in range(helicities):
         mask = active_row(counts_ref, h, width)
@@ -213,7 +212,9 @@
         previous = prev_ref[h] if final else prev_ref[h].T * mask
         out_ref[h] = damp * (2.0 * (mask * total) - damp * previous)
         if final:
-            refs[0][h] = field.T
+            refs[AHEAD][h] = field.T
+    for copy in ahead:
+        copy.wait()
 
 
 def renew(h, got_ref, counts_ref, local_ref, columns, cent_ref, damp_ref, cor_ref, inner_ref, outer_ref, kept_ref, arrived):
@@ -232,39 +233,42 @@
         above = jnp.where(odd_group(), outer_ref[...], inner_ref[...])
         total = total - cent_ref[...] * (above.astype(F32) * cor_ref[h : h + 1, :])
     sources = [slot.astype(BF) for slot in slots[:-1]]
-    total = forward(sources, [kept_ref.at[h, j] for j in range(SIDES)], columns, total, arrived[h])
+    total = forward(sources, [kept_ref.at[j] for j in range(SIDES)], columns, total, arrived[h])
     return local_ref[h] + 2.0 * damp_ref[...] * (active_row(counts_ref, h, width) * total)
 
 
 def middle_kernel(
-    counts_ref, radial_ref, cent_ref, damp_ref, cor_ref, got_ref, local_ref, inner_got, outer_got, blocks_ref,
-    field_ref, inner_ref, outer_ref, send_ref, columns, kept_ref, made_ref, edge_ref, block_sem, edge_sem, send_sem,
+    counts_ref, columns, cent_ref, damp_ref, cor_ref, got_ref, local_ref, inner_got, outer_got, *refs
 ):
-    arrived = fetch(blocks_ref, kept_ref, block_sem)
-    radial_columns(radial_ref, columns)
+    blocks_ref, field_ref, inner_ref, outer_ref, send_ref, kept_ref, made_ref, edge_ref, block_sem, edge_sem, send_sem = refs[
+        AHEAD:
+    ]
+    arrived = fetch(blocks_ref, kept_ref, block_sem, AHEAD)
+    mine = list(refs[:AHEAD]) + [kept_ref.at[h] for h in range(AHEAD, local_ref.shape[0])]
     sent = []
     for h in range(local_ref.shape[0]):
         field = renew(
-            h, got_ref, counts_ref, local_ref, columns, cent_ref, damp_ref, cor_ref, inner_got, outer_got, kept_ref, arrived
+            h, got_ref, counts_ref, local_ref, columns, cent_ref, damp_ref, cor_ref, inner_got, outer_got, mine[h], arrived
         )
         field_ref[h] = field
-        emit_products(field, kept_ref.at[h], columns, made_ref.at[h])
+        if h + 1 == field_ref.shape[0]:
+            sent += emit_edges(field_ref, cor_ref, edge_ref, inner_ref, outer_ref, edge_sem)
+        emit_products(field, mine[h], columns, made_ref.at[h])
         sent.append(copy_out(h, made_ref, send_ref, send_sem))
-    sent += emit_edges(field_ref, cor_ref, edge_ref, inner_ref, outer_ref, edge_sem)
     for copy in sent:
         copy.wait()
 
 
 def last_kernel(
-    counts_ref, radial_ref, cent_ref, damp_ref, cor_ref, got_ref, local_ref, inner_got, outer_got, blocks_ref, out_ref,
-    columns, kept_ref, made_ref, block_sem, sem,
+    counts_ref, columns, cent_ref, damp_ref, cor_ref, got_ref, local_ref, inner_got, outer_got, *refs
 ):
-    arrived = fetch(blocks_ref, kept_ref, block_sem)
-    radial_columns(radial_ref, columns)
+    blocks_ref, out_ref, kept_ref, made_ref, block_sem, sem = refs[AHEAD:]
+    arrived = fetch(blocks_ref, kept_ref, block_sem, AHEAD)
+    mine = list(refs[:AHEAD]) + [kept_ref.at[h] for h in range(AHEAD, local_ref.shape[0])]
     sent = []
     for h in range(local_ref.shape[0]):
         field = renew(
-            h, got_ref, counts_ref, local_ref, columns, cent_ref, damp_ref, cor_ref, inner_got, outer_got, kept_ref, arrived
+            h, got_ref, counts_ref, local_ref, columns, cent_ref, damp_ref, cor_ref, inner_got, outer_got, mine[h], arrived
         )
         made_ref[h] = field.T
         copy = pltpu.make_async_copy(made_ref.at[h], out_ref.at[h], sem.at[h])
@@ -309,9 +313,9 @@
     pair = pltpu.SemaphoreType.DMA((2,))
     columns = pltpu.VMEM((terms, points, width), F32)
     made = pltpu.VMEM((helicities, count, rows, width), BF)
+    ahead_out = pltpu.VMEM((SIDES,) + blocks.shape[3:], BF)
     kept = pltpu.VMEM((helicities, SIDES) + blocks.shape[3:], BF)
     copies = pltpu.SemaphoreType.DMA((helicities,))
-    parts = pltpu.SemaphoreType.DMA((helicities, (SIDES + 1) // 2))
     diagonal = pl.BlockSpec((helicities, 1, 1) + blocks.shape[3:], lambda *_: (0,) * blocks.ndim)
     mac = 2 * helicities * points * width * width * terms
 
@@ -336,7 +340,7 @@
         blocks.size * 2,
         [
             pltpu.VMEM(psi_cur.shape, F32), pltpu.VMEM(radial_terms.shape, F32), pltpu.VMEM(coriolis.shape, F32), columns, kept,
-            made, edges, pair, copies, parts, pair, copies,
+            made, edges, pair, copies, copies, pair, copies,
         ],
     )
     route = call(
@@ -354,11 +358,11 @@
         tables = [whole(a) for a in (psi_prev, radial_terms, kinetic, cent, damp, energies, rotation, coriolis)]
         if final:
             tables[0] = vmem
-        out_specs = [vmem, whole(psi_prev)] if final else vmem
-        out_shape = [field_out, pltpu.HBM(psi_prev.shape, F32)] if final else field_out
-        return call(kernel, [smem] + tables + [vmem, diagonal], out_specs, out_shape, 2 * mac, 4 * psi_cur.size, [columns])
-
-    given = [smem] + [vmem] * 8 + [hbm]
+        out_specs = [vmem] * (2 + AHEAD) + [whole(psi_prev)] * final
+        out_shape = [field_out, columns] + [ahead_out] * AHEAD + [pltpu.HBM(psi_prev.shape, F32)] * final
+        return call(kernel, [smem] + tables + [vmem, diagonal, hbm], out_specs, out_shape, 2 * mac, 4 * psi_cur.size, [copies])
+
+    given = [smem] + [vmem] * (8 + AHEAD) + [hbm]
     middle = call(
         middle_kernel,
         given,
@@ -366,7 +370,7 @@
         [field_out, edge_out, edge_out, parcel_out],
         2 * SIDES * mac,
         blocks.size,
-        [columns, kept, made, edges, parts, pair, copies],
+        [kept, made, edges, copies, pair, copies],
     )
     final = call(
         last_kernel,
@@ -375,7 +379,7 @@
         pltpu.HBM(psi_cur.shape, F32),
         SIDES * mac,
         blocks.size,
-        [columns, kept, pltpu.VMEM(psi_cur.shape, F32), parts, copies],
+        [kept, pltpu.VMEM(psi_cur.shape, F32), copies, copies],
     )
 
     field, inner, outer, send = first(counts, place(radial_terms), place(coriolis), psi_cur, blocks)
@@ -386,14 +390,14 @@
         outer = swapped(outer, "hel", 1)
         inner = swapped(inner, "hel", 0)
         rest = local(iteration > 0)(
-            counts, prev, radial_terms, kinetic, cent, damp, energies, rotation, coriolis, field, blocks
+            counts, prev, radial_terms, kinetic, cent, damp, energies, rotation, coriolis, field, blocks, blocks
         )
+        rest, spread, *more = rest
+        ahead, before = more[:AHEAD], more[AHEAD:]
+        back = exchange(route(offsets, got, rest, inner, outer))
+        given = (counts, spread, cent, damp, coriolis, back, rest, inner, outer, *ahead, blocks)
         if ends:
-            rest, before = rest
-        back = exchange(route(offsets, got, rest, inner, outer))
-        given = (counts, radial_terms, cent, damp, coriolis, back, rest, inner, outer, blocks)
-        if ends:
-            return before, final(*given)
+            return before[0], final(*given)
         prev = field
         field, inner, outer, send = middle(*given)
 

time: 146 us -> 142 us (0.973)
  waiting for transfers between devices: 39.2 us -> 24.9 us
  local copies, waits for them, and re-layouts: 0.06 us -> 9.65 us
    all_to_all x2, waiting for transfers between devices: 39.2 us -> 24.9 us  [exchange(): return lax.all_to_all(x, 'chan', 0, 0, tiled=True)]
    unnamed x20 -> x52, local copies, waits for them, and re-layouts: 0.06 us -> 9.65 us
    pallas_call x2, Pallas kernels: 6.78 us -> 11.5 us  [body(): local(iteration > 0)]
    pallas_call x1, Pallas kernels: 5.49 us -> 3.32 us  [body(): return (before[0], final(*given))]
    pallas_call x1, Pallas kernels: 7.68 us -> 5.67 us  [body(): field, inner, outer, send = middle(*given)]
  transfers between devices with their start and end apart: 6 -> 6, of which waited for: 2 -> 2; matrix products, arithmetic and copies ran while one was open for 0% -> 0% of each run, Pallas kernels for 5% -> 8%
where the time goes in v4:
time: 142 us
  blocking collectives  58.1 us (41%)
  Pallas kernels  30.6 us (22%)
  waiting for transfers between devices  24.9 us (18%)
  starting transfers between devices  17.4 us (12%)
  local copies, waits for them, and re-layouts  9.65 us (7%)
    all_to_all x2, blocking collectives, exchange(): return lax.all_to_all(x, 'chan', 0, 0, tiled=True)  58.1 us
    all_to_all x2, waiting for transfers between devices, exchange(): return lax.all_to_all(x, 'chan', 0, 0, tiled=True)  24.9 us
    all_to_all x2, starting transfers between devices, exchange(): return lax.all_to_all(x, 'chan', 0, 0, tiled=True)  15.7 us
    pallas_call x2, Pallas kernels, body(): local(iteration > 0)  11.5 us
    unnamed x52, local copies, waits for them, and re-layouts  9.65 us
    pallas_call x1, Pallas kernels, body(): first(counts, place(radial_terms), place(coriolis), psi_cur, blocks)  6.61 us
    pallas_call x1, Pallas kernels, body(): field, inner, outer, send = middle(*given)  5.67 us
    pallas_call x2, Pallas kernels, body(): back = exchange(route(offsets, got, rest, inner, outer))  3.47 us
  transfers between devices with their start and end apart: 6, of which 2 were waited for; matrix products, arithmetic and copies ran while one was open for 0% of the time, Pallas kernels for 8%

profile of v4, /device:TPU:0, one launch (start us, length us, event | category | flops | bytes accessed | tf_op | source)
XLA Modules:
  0.0 141.8 jit_solution(469891985484335360)
XLA Ops:
  0.6 6.6 %shard_map.131 = (f32[3,256,128]{2,1,0:T(8,128)S(1)}, bf16[256,128]{1,0:T(8,128)(2,1)}, bf16[256,128]{1,0:T(8,128)(2,1)}, bf16[32,192,128]{2,1,0:T(8,128)(2,1)}) custom-call(s32[3]{0:T(128)} %counts_ref.9, f32[8,256]{1,0:T(8,128)} %radial_ref.3, f32[3,128]{1,0:T(4,128)} %cor_ref.7, f32[3,128,256]{2,1,0:T(8,128)} %psi_ref.1, ...), custom_call_target="tpu_custom_call" | custom-call | flops 1409286144 | bytes 6291456 | tf_op jit(solution)/shard_map/pallas_call | solution.py:385
  7.2 0.0 copy-start.25
  7.3 0.0 copy-start.24
  7.3 0.0 copy-start
  7.3 0.0 copy-start.1
  7.3 0.0 copy-start.18
  7.3 0.0 copy-start.19
  7.3 0.0 copy-start.20
  7.3 0.0 copy-start.21
  7.3 0.0 copy-start.22
  7.4 10.9 %all-to-all-start = ((bf16[32,192,128]{2,1,0:T(8,128)(2,1)}), bf16[32,192,128]{2,1,0:T(8,128)(2,1)S(1)}, u32[]{:S(2)}, u32[]{:S(2)}) async-start(bf16[32,192,128]{2,1,0:T(8,128)(2,1)} %get-tuple-element.23), calls=%async_computation | async-start | bytes 3145728 | tf_op jit(solution)/shard_map/all_to_all | solution.py:288
  18.2 0.0 copy-done.25
  18.2 0.1 collective-permute-start
  18.3 0.0 copy-done.24
  18.3 0.7 collective-permute-start.1
  19.0 0.0 copy-done
  19.0 0.0 copy-done.1
  19.0 0.0 copy-done.18
  19.0 0.0 copy-done.19
  19.1 0.0 copy-done.20
  19.1 5.2 %shard_map.132 = (f32[3,256,128]{2,1,0:T(8,128)S(1)}, f32[8,256,128]{2,1,0:T(8,128)S(1)}, bf16[7,8,128,128]{3,2,1,0:T(8,128)(2,1)S(1)}, bf16[7,8,128,128]{3,2,1,0:T(8,128)(2,1)S(1)}, bf16[7,8,128,128]{3,2,1,0:T(8,128)(2,1)S(1)}) custom-call(s32[3]{0:T(128)} %counts_ref.9, f32[3,128,256]{2,1,0:T(8,128)} %prev_ref.1, f32[8,256]{1,0:T(8,128)S(1)} %copy-done.19, ...), custom_call_target="tpu_custom_call" | custom-call | flops 402653184 | bytes 393216 | tf_op jit(solution)/shard_map/pallas_call | solution.py:392
  24.3 1.2 copy-done.8
  25.5 1.2 copy-done.10
  26.7 1.3 copy-done.12
  28.0 1.1 copy-done.16
  29.0 0.0 collective-permute-done.refs_1_.inner_got
  29.0 0.0 collective-permute-done.1.refs_2_.outer_got
  29.1 12.9 %all-to-all-done.got_ref = bf16[32,192,128]{2,1,0:T(8,128)(2,1)S(1)} async-done(((bf16[32,192,128]{2,1,0:T(8,128)(2,1)}), bf16[32,192,128]{2,1,0:T(8,128)(2,1)S(1)}, u32[]{:S(2)}, u32[]{:S(2)}) %all-to-all-start) | async-done | bytes 1572896 | tf_op jit(solution)/shard_map/all_to_all | solution.py:288
  42.0 1.7 %shard_map.133 = bf16[32,192,128]{2,1,0:T(8,128)(2,1)S(1)} custom-call(s32[3,7]{1,0:T(4,128)} %offsets_ref.3, bf16[32,192,128]{2,1,0:T(8,128)(2,1)S(1)} %all-to-all-done.got_ref, f32[3,256,128]{2,1,0:T(8,128)S(1)} %get-tuple-element.24.refs_0_.local_ref, bf16[256,128]{1,0:T(8,128)(2,1)S(1)} %collective-permute-done.refs_1_.inner_got, ...), custom_call_target="tpu_custom_call" | custom-call | flops 786432 | bytes 393216 | tf_op jit(solution)/shard_map/pallas_call | solution.py:397
  43.8 29.6 %all_to_all.20.got_ref = bf16[32,192,128]{2,1,0:T(8,128)(2,1)S(1)} all-to-all(bf16[32,192,128]{2,1,0:T(8,128)(2,1)S(1)} %shard_map.133), channel_id=1, replica_groups=mesh['chan'=32,'hel'=4] {'chan'}, dimensions={0} | all-to-all | bytes 3145728 | tf_op jit(solution)/shard_map/all_to_all | solution.py:288
  73.4 0.0 copy-done.13
  73.4 5.7 %shard_map.134 = (f32[3,256,128]{2,1,0:T(8,128)S(1)}, bf16[256,128]{1,0:T(8,128)(2,1)}, bf16[256,128]{1,0:T(8,128)(2,1)}, bf16[32,192,128]{2,1,0:T(8,128)(2,1)}) custom-call(s32[3]{0:T(128)} %counts_ref.9, f32[8,256,128]{2,1,0:T(8,128)S(1)} %copy-done.17, f32[256,128]{1,0:T(8,128)S(1)} %copy-done.1, f32[256,128]{1,0:T(8,128)S(1)} %copy-done, ...), custom_call_target="tpu_custom_call" | custom-call | flops 2818572288 | bytes 3145728 | tf_op jit(solution)/shard_map/pallas_call | solution.py:402
  79.1 0.0 copy-start.23
  79.1 4.8 %all-to-all-start.2 = ((bf16[32,192,128]{2,1,0:T(8,128)(2,1)}), bf16[32,192,128]{2,1,0:T(8,128)(2,1)S(1)}, u32[]{:S(2)}, u32[]{:S(2)}) async-start(bf16[32,192,128]{2,1,0:T(8,128)(2,1)} %get-tuple-element.33), calls=%async_computation.2 | async-start | bytes 3145728 | tf_op jit(solution)/shard_map/all_to_all | solution.py:288
  83.9 0.1 collective-permute-start.2
  84.1 0.8 collective-permute-start.3
  84.9 6.4 %shard_map.135 = (f32[3,256,128]{2,1,0:T(8,128)S(1)}, f32[8,256,128]{2,1,0:T(8,128)S(1)}, bf16[7,8,128,128]{3,2,1,0:T(8,128)(2,1)S(1)}, bf16[7,8,128,128]{3,2,1,...) custom-call(s32[3]{0:T(128)} %counts_ref.9, ...), custom_call_target="tpu_custom_call" | custom-call | flops 402653184 | bytes 393216 | tf_op jit(solution)/shard_map/pallas_call | solution.py:392
  91.3 1.2 copy-done.2
  92.5 1.2 copy-done.4
  93.7 1.3 copy-done.6
  95.0 1.1 copy-done.14
  96.1 0.0 collective-permute-done.2.refs_1_.inner_got
  96.1 0.0 collective-permute-done.3.refs_2_.outer_got
  96.1 11.9 %all-to-all-done.2.got_ref = bf16[32,192,128]{2,1,0:T(8,128)(2,1)S(1)} async-done(((bf16[32,192,128]{2,1,0:T(8,128)(2,1)}), bf16[32,192,128]{2,1,0:T(8,128)(2,1)S(1)}, u32[]{:S(2)}, u32[]{:S(2)}) %all-to-all-start.2) | async-done | bytes 1572896 | tf_op jit(solution)/shard_map/all_to_all | solution.py:288
  108.0 1.7 %shard_map.136 = bf16[32,192,128]{2,1,0:T(8,128)(2,1)S(1)} custom-call(s32[3,7]{1,0:T(4,128)} %offsets_ref.3, bf16[32,192,128]{2,1,0:T(8,128)(2,1)S(1)} %all-to-all-done.2.got_ref, f32[3,256,128]{2,1,0:T(8,128)S(1)} %get-tuple-element.34.refs_0_.local_ref, bf16[256,128]{1,0:T(8,128)(2,1)S(1)} %collective-permute-done.2.refs_1_.inner_got, ...), custom_call_target="tpu_custom_call" | custom-call | flops 786432 | bytes 393216 | tf_op jit(solution)/shard_map/pallas_call | solution.py:397
  109.8 28.5 %all_to_all.21.got_ref = bf16[32,192,128]{2,1,0:T(8,128)(2,1)S(1)} all-to-all(bf16[32,192,128]{2,1,0:T(8,128)(2,1)S(1)} %shard_map.136), channel_id=1, replica_groups=mesh['chan'=32,'hel'=4] {'chan'}, dimensions={0} | all-to-all | bytes 3145728 | tf_op jit(solution)/shard_map/all_to_all | solution.py:288
  138.3 0.0 copy-done.5
  138.3 3.3 %shard_map.137 = f32[3,128,256]{2,1,0:T(8,128)} custom-call(s32[3]{0:T(128)} %counts_ref.9, f32[8,256,128]{2,1,0:T(8,128)S(1)} %copy-done.15, f32[256,128]{1,0:T(8,128)S(1)} %copy-done.1, f32[256,128]{1,0:T(8,128)S(1)} %copy-done, f32[3,128]{1,0:T(4,128)S(1)} %copy-done.20, bf16[32,192,128]{2,1,0:T(8,128)(2,1)S(1)} %all_to_all.21.got_ref, ...), custom_call_target="tpu_custom_call" | custom-call | flops 1409286144 | bytes 3145728 | tf_op jit(solution)/shard_map/pallas_call | solution.py:400
  (25 shorter events, 0.0 us)
Async XLA Ops:
  7.2 11.0 %copy-start.25 = (bf16[256,128]{1,0:T(8,128)(2,1)S(1)}, bf16[256,128]{1,0:T(8,128)(2,1)}, u32[]{:S(2)}) copy-start(bf16[256,128]{1,0:T(8,128)(2,1)} %get-tuple-element.25) | copy-start | bytes 196612
  7.3 11.1 %copy-start.24 = (bf16[256,128]{1,0:T(8,128)(2,1)S(1)}, bf16[256,128]{1,0:T(8,128)(2,1)}, u32[]{:S(2)}) copy-start(bf16[256,128]{1,0:T(8,128)(2,1)} %get-tuple-element.26) | copy-start | bytes 196612
  7.3 11.7 %copy-start = (f32[256,128]{1,0:T(8,128)S(1)}, f32[256,128]{1,0:T(8,128)}, u32[]{:S(2)}) copy-start(f32[256,128]{1,0:T(8,128)} %constant.8.clone.damp_ref) | copy-start | bytes 393220
  7.3 11.7 %copy-start.1 = (f32[256,128]{1,0:T(8,128)S(1)}, f32[256,128]{1,0:T(8,128)}, u32[]{:S(2)}) copy-start(f32[256,128]{1,0:T(8,128)} %constant.7.clone.cent_ref) | copy-start | bytes 393220
  7.3 11.7 %copy-start.18 = (f32[256,256]{1,0:T(8,128)S(1)}, f32[256,256]{1,0:T(8,128)}, u32[]{:S(2)}) copy-start(f32[256,256]{1,0:T(8,128)} %constant.6.clone.kin_ref) | copy-start | bytes 786436
  7.3 11.7 %copy-start.19 = (f32[8,256]{1,0:T(8,128)S(1)}, f32[8,256]{1,0:T(8,128)}, u32[]{:S(2)}) copy-start(f32[8,256]{1,0:T(8,128)} %radial_ref.3) | copy-start | bytes 24580
  7.3 11.7 %copy-start.20 = (f32[3,128]{1,0:T(4,128)S(1)}, f32[3,128]{1,0:T(4,128)}, u32[]{:S(2)}) copy-start(f32[3,128]{1,0:T(4,128)} %cor_ref.7) | copy-start | bytes 4612
  7.3 11.7 %copy-start.21 = (f32[3,128]{1,0:T(4,128)S(1)}, f32[3,128]{1,0:T(4,128)}, u32[]{:S(2)}) copy-start(f32[3,128]{1,0:T(4,128)} %e_ref.3) | copy-start | bytes 4612
  7.3 11.7 %copy-start.22 = (f32[3,128]{1,0:T(4,128)S(1)}, f32[3,128]{1,0:T(4,128)}, u32[]{:S(2)}) copy-start(f32[3,128]{1,0:T(4,128)} %rot_ref.3) | copy-start | bytes 4612
  7.4 34.6 %all-to-all-start = ((bf16[32,192,128]{2,1,0:T(8,128)(2,1)}), bf16[32,192,128]{2,1,0:T(8,128)(2,1)S(1)}, u32[]{:S(2)}, u32[]{:S(2)}) async-start(bf16[32,192,128]{2,1,0:T(8,128)(2,1)} %get-tuple-element.23), calls=%async_computation | async-start | bytes 3145728 | tf_op jit(solution)/shard_map/all_to_all | solution.py:288
  18.2 10.8 %collective-permute-start = (bf16[256,128]{1,0:T(8,128)(2,1)S(1)}, bf16[256,128]{1,0:T(8,128)(2,1)S(1)}, u32[]{:S(2)}, u32[]{:S(2)}) collective-permute-start(bf16[256,128]{1,0:T(8,128)(2,1)S(1)} %copy-done.25), channel_id=1, source_target_pairs={{0,1},{2,3},{1,0},{3,2},{4,5},{6,7},{5,4},{7,6},{8,9},{10,11},{9,8... | collective-permute-start | bytes 196616 | tf_op jit(solution)/shard_map/ppermute | solution.py:284
  18.3 10.7 %collective-permute-start.1 = (bf16[256,128]{1,0:T(8,128)(2,1)S(1)}, bf16[256,128]{1,0:T(8,128)(2,1)S(1)}, u32[]{:S(2)}, u32[]{:S(2)}) collective-permute-start(bf16[256,128]{1,0:T(8,128)(2,1)S(1)} %copy-done.24), channel_id=1, source_target_pairs={{1,2},{2,1},{5,6},{6,5},{9,10},{10,9},{13,14},{14,13},{17,18},{18,... | collective-permute-start | bytes 196616 | tf_op jit(solution)/shard_map/ppermute | solution.py:284
  24.3 1.2 copy-start.8
  25.5 1.2 copy-start.10
  26.7 1.3 copy-start.12
  28.0 1.1 copy-start.16
  42.0 31.4 %copy-start.11 = (bf16[7,8,128,128]{3,2,1,0:T(8,128)(2,1)S(1)}, bf16[7,8,128,128]{3,2,1,0:T(8,128)(2,1)}, u32[]{:S(2)}) copy-start(bf16[7,8,128,128]{3,2,1,0:T(8,128)(2,1)} %copy-done.10) | copy-start | bytes 5505028
  42.0 31.4 %copy-start.13 = (bf16[7,8,128,128]{3,2,1,0:T(8,128)(2,1)S(1)}, bf16[7,8,128,128]{3,2,1,0:T(8,128)(2,1)}, u32[]{:S(2)}) copy-start(bf16[7,8,128,128]{3,2,1,0:T(8,128)(2,1)} %copy-done.12) | copy-start | bytes 5505028
  43.7 29.7 %copy-start.9 = (bf16[7,8,128,128]{3,2,1,0:T(8,128)(2,1)S(1)}, bf16[7,8,128,128]{3,2,1,0:T(8,128)(2,1)}, u32[]{:S(2)}) copy-start(bf16[7,8,128,128]{3,2,1,0:T(8,128)(2,1)} %copy-done.8) | copy-start | bytes 5505028
  43.7 29.7 %copy-start.17 = (f32[8,256,128]{2,1,0:T(8,128)S(1)}, f32[8,256,128]{2,1,0:T(8,128)}, u32[]{:S(2)}) copy-start(f32[8,256,128]{2,1,0:T(8,128)} %copy-done.16) | copy-start | bytes 3145732
  79.1 5.0 %copy-start.23 = (bf16[256,128]{1,0:T(8,128)(2,1)S(1)}, bf16[256,128]{1,0:T(8,128)(2,1)}, u32[]{:S(2)}) copy-start(bf16[256,128]{1,0:T(8,128)(2,1)} %get-tuple-element.36) | copy-start | bytes 196612
  79.1 28.9 %all-to-all-start.2 = ((bf16[32,192,128]{2,1,0:T(8,128)(2,1)}), bf16[32,192,128]{2,1,0:T(8,128)(2,1)S(1)}, u32[]{:S(2)}, u32[]{:S(2)}) async-start(bf16[32,192,128]{2,1,0:T(8,128)(2,1)} %get-tuple-element.33), calls=%async_computation.2 | async-start | bytes 3145728 | tf_op jit(solution)/shard_map/all_to_all | solution.py:288
  83.9 12.1 %collective-permute-start.2 = (bf16[256,128]{1,0:T(8,128)(2,1)}, bf16[256,128]{1,0:T(8,128)(2,1)S(1)}, u32[]{:S(2)}, u32[]{:S(2)}) collective-permute-start(bf16[256,128]{1,0:T(8,128)(2,1)} %get-tuple-element.35), channel_id=1, source_target_pairs={{0,1},{2,3},{1,0},{3,2},{4,5},{6,7},{5,4},{7,6},{8,9},{10,11},{9,8... | collective-permute-start | bytes 196616 | tf_op jit(solution)/shard_map/ppermute | solution.py:284
  84.1 12.0 %collective-permute-start.3 = (bf16[256,128]{1,0:T(8,128)(2,1)S(1)}, bf16[256,128]{1,0:T(8,128)(2,1)S(1)}, u32[]{:S(2)}, u32[]{:S(2)}) collective-permute-start(bf16[256,128]{1,0:T(8,128)(2,1)S(1)} %copy-done.23), channel_id=1, source_target_pairs={{1,2},{2,1},{5,6},{6,5},{9,10},{10,9},{13,14},{14,13},{17,18},{18,... | collective-permute-start | bytes 196616 | tf_op jit(solution)/shard_map/ppermute | solution.py:284
  91.3 1.2 copy-start.2
  92.5 1.2 copy-start.4
  93.7 1.3 copy-start.6
  95.0 1.1 copy-start.14
  108.0 30.3 %copy-start.5 = (bf16[7,8,128,128]{3,2,1,0:T(8,128)(2,1)S(1)}, bf16[7,8,128,128]{3,2,1,0:T(8,128)(2,1)}, u32[]{:S(2)}) copy-start(bf16[7,8,128,128]{3,2,1,0:T(8,128)(2,1)} %copy-done.4) | copy-start | bytes 5505028
  108.0 30.3 %copy-start.7 = (bf16[7,8,128,128]{3,2,1,0:T(8,128)(2,1)S(1)}, bf16[7,8,128,128]{3,2,1,0:T(8,128)(2,1)}, u32[]{:S(2)}) copy-start(bf16[7,8,128,128]{3,2,1,0:T(8,128)(2,1)} %copy-done.6) | copy-start | bytes 5505028
  109.7 28.5 %copy-start.3 = (bf16[7,8,128,128]{3,2,1,0:T(8,128)(2,1)S(1)}, bf16[7,8,128,128]{3,2,1,0:T(8,128)(2,1)}, u32[]{:S(2)}) copy-start(bf16[7,8,128,128]{3,2,1,0:T(8,128)(2,1)} %copy-done.2) | copy-start | bytes 5505028
  109.8 28.5 %copy-start.15 = (f32[8,256,128]{2,1,0:T(8,128)S(1)}, f32[8,256,128]{2,1,0:T(8,128)}, u32[]{:S(2)}) copy-start(f32[8,256,128]{2,1,0:T(8,128)} %copy-done.14) | copy-start | bytes 3145732

commit v5 on v4

--- a/solution.py
+++ b/solution.py
@@ -120,9 +120,11 @@
         pltpu.make_async_copy(radial_hbm, radial_ref, small_sem.at[0]),
         pltpu.make_async_copy(cor_hbm, cor_ref, small_sem.at[1]),
     ]
-    for copy in small + psi:
+    for copy in small + psi[:1]:
         copy.start()
     arrived = fetch(blocks_ref, kept_ref, block_sem)
+    for copy in psi[1:]:
+        copy.start()
     for copy in small:
         copy.wait()
     radial_columns(radial_ref, columns_ref)

time: 142 us -> 142 us (level)
  no operation moved by 1% of the time
where the time goes in v5:
time: 142 us
  blocking collectives  58.1 us (41%)
  Pallas kernels  30.6 us (22%)
  waiting for transfers between devices  24.9 us (18%)
  starting transfers between devices  17.4 us (12%)
  local copies, waits for them, and re-layouts  9.65 us (7%)
    all_to_all x2, blocking collectives, exchange(): return lax.all_to_all(x, 'chan', 0, 0, tiled=True)  58.1 us
    all_to_all x2, waiting for transfers between devices, exchange(): return lax.all_to_all(x, 'chan', 0, 0, tiled=True)  24.9 us
    all_to_all x2, starting transfers between devices, exchange(): return lax.all_to_all(x, 'chan', 0, 0, tiled=True)  15.7 us
    pallas_call x2, Pallas kernels, body(): local(iteration > 0)  11.5 us
    unnamed x52, local copies, waits for them, and re-layouts  9.65 us
    pallas_call x1, Pallas kernels, body(): first(counts, place(radial_terms), place(coriolis), psi_cur, blocks)  6.61 us
    pallas_call x1, Pallas kernels, body(): field, inner, outer, send = middle(*given)  5.66 us
    pallas_call x2, Pallas kernels, body(): back = exchange(route(offsets, got, rest, inner, outer))  3.47 us
  transfers between devices with their start and end apart: 6, of which 2 were waited for; matrix products, arithmetic and copies ran while one was open for 0% of the time, Pallas kernels for 8%

profile of v5, /device:TPU:0, one launch (start us, length us, event | category | flops | bytes accessed | tf_op | source)
XLA Modules:
  0.0 141.8 jit_solution(6627422789175225358)
XLA Ops:
  0.6 6.6 %shard_map.131 = (f32[3,256,128]{2,1,0:T(8,128)S(1)}, bf16[256,128]{1,0:T(8,128)(2,1)}, bf16[256,128]{1,0:T(8,128)(2,1)}, bf16[32,192,128]{2,1,0:T(8,128)(2,1)}) custom-call(s32[3]{0:T(128)} %counts_ref.9, f32[8,256]{1,0:T(8,128)} %radial_ref.3, f32[3,128]{1,0:T(4,128)} %cor_ref.7, f32[3,128,256]{2,1,0:T(8,128)} %psi_ref.1, ...), custom_call_target="tpu_custom_call" | custom-call | flops 1409286144 | bytes 6291456 | tf_op jit(solution)/shard_map/pallas_call | solution.py:387
  7.2 0.0 copy-start.25
  7.3 0.0 copy-start.24
  7.3 0.0 copy-start
  7.3 0.0 copy-start.1
  7.3 0.0 copy-start.18
  7.3 0.0 copy-start.19
  7.3 0.0 copy-start.20
  7.3 0.0 copy-start.21
  7.3 0.0 copy-start.22
  7.4 10.9 %all-to-all-start = ((bf16[32,192,128]{2,1,0:T(8,128)(2,1)}), bf16[32,192,128]{2,1,0:T(8,128)(2,1)S(1)}, u32[]{:S(2)}, u32[]{:S(2)}) async-start(bf16[32,192,128]{2,1,0:T(8,128)(2,1)} %get-tuple-element.23), calls=%async_computation | async-start | bytes 3145728 | tf_op jit(solution)/shard_map/all_to_all | solution.py:290
  18.2 0.0 copy-done.25
  18.2 0.1 collective-permute-start
  18.3 0.0 copy-done.24
  18.3 0.7 collective-permute-start.1
  19.0 0.0 copy-done
  19.0 0.0 copy-done.1
  19.1 5.2 %shard_map.132 = (f32[3,256,128]{2,1,0:T(8,128)S(1)}, f32[8,256,128]{2,1,0:T(8,128)S(1)}, bf16[7,8,128,128]{3,2,1,0:T(8,128)(2,1)S(1)}, bf16[7,8,128,128]{3,2,1,0:T(8,128)(2,1)S(1)}, bf16[7,8,128,128]{3,2,1,0:T(8,128)(2,1)S(1)}) custom-call(s32[3]{0:T(128)} %counts_ref.9, f32[3,128,256]{2,1,0:T(8,128)} %prev_ref.1, f32[8,256]{1,0:T(8,128)S(1)} %copy-done.19, ...), custom_call_target="tpu_custom_call" | custom-call | flops 402653184 | bytes 393216 | tf_op jit(solution)/shard_map/pallas_call | solution.py:394
  24.3 1.2 copy-done.8
  25.5 1.2 copy-done.10
  26.7 1.3 copy-done.12
  28.0 1.1 copy-done.16
  29.0 0.0 collective-permute-done.refs_1_.inner_got
  29.0 0.0 collective-permute-done.1.refs_2_.outer_got
  29.1 12.9 %all-to-all-done.got_ref = bf16[32,192,128]{2,1,0:T(8,128)(2,1)S(1)} async-done(((bf16[32,192,128]{2,1,0:T(8,128)(2,1)}), bf16[32,192,128]{2,1,0:T(8,128)(2,1)S(1)}, u32[]{:S(2)}, u32[]{:S(2)}) %all-to-all-start) | async-done | bytes 1572896 | tf_op jit(solution)/shard_map/all_to_all | solution.py:290
  42.0 1.7 %shard_map.133 = bf16[32,192,128]{2,1,0:T(8,128)(2,1)S(1)} custom-call(s32[3,7]{1,0:T(4,128)} %offsets_ref.3, bf16[32,192,128]{2,1,0:T(8,128)(2,1)S(1)} %all-to-all-done.got_ref, f32[3,256,128]{2,1,0:T(8,128)S(1)} %get-tuple-element.24.refs_0_.local_ref, bf16[256,128]{1,0:T(8,128)(2,1)S(1)} %collective-permute-done.refs_1_.inner_got, ...), custom_call_target="tpu_custom_call" | custom-call | flops 786432 | bytes 393216 | tf_op jit(solution)/shard_map/pallas_call | solution.py:399
  43.7 29.6 %all_to_all.20.got_ref = bf16[32,192,128]{2,1,0:T(8,128)(2,1)S(1)} all-to-all(bf16[32,192,128]{2,1,0:T(8,128)(2,1)S(1)} %shard_map.133), channel_id=1, replica_groups=mesh['chan'=32,'hel'=4] {'chan'}, dimensions={0} | all-to-all | bytes 3145728 | tf_op jit(solution)/shard_map/all_to_all | solution.py:290
  73.4 0.0 copy-done.13
  73.4 5.7 %shard_map.134 = (f32[3,256,128]{2,1,0:T(8,128)S(1)}, bf16[256,128]{1,0:T(8,128)(2,1)}, bf16[256,128]{1,0:T(8,128)(2,1)}, bf16[32,192,128]{2,1,0:T(8,128)(2,1)}) custom-call(s32[3]{0:T(128)} %counts_ref.9, f32[8,256,128]{2,1,0:T(8,128)S(1)} %copy-done.17, f32[256,128]{1,0:T(8,128)S(1)} %copy-done.1, f32[256,128]{1,0:T(8,128)S(1)} %copy-done, ...), custom_call_target="tpu_custom_call" | custom-call | flops 2818572288 | bytes 3145728 | tf_op jit(solution)/shard_map/pallas_call | solution.py:404
  79.1 0.0 copy-start.23
  79.1 4.9 %all-to-all-start.2 = ((bf16[32,192,128]{2,1,0:T(8,128)(2,1)}), bf16[32,192,128]{2,1,0:T(8,128)(2,1)S(1)}, u32[]{:S(2)}, u32[]{:S(2)}) async-start(bf16[32,192,128]{2,1,0:T(8,128)(2,1)} %get-tuple-element.33), calls=%async_computation.2 | async-start | bytes 3145728 | tf_op jit(solution)/shard_map/all_to_all | solution.py:290
  84.0 0.1 collective-permute-start.2
  84.1 0.8 collective-permute-start.3
  84.9 6.4 %shard_map.135 = (f32[3,256,128]{2,1,0:T(8,128)S(1)}, f32[8,256,128]{2,1,0:T(8,128)S(1)}, bf16[7,8,128,128]{3,2,1,0:T(8,128)(2,1)S(1)}, bf16[7,8,128,128]{3,2,1,...) custom-call(s32[3]{0:T(128)} %counts_ref.9, ...), custom_call_target="tpu_custom_call" | custom-call | flops 402653184 | bytes 393216 | tf_op jit(solution)/shard_map/pallas_call | solution.py:394
  91.3 1.2 copy-done.2
  92.5 1.2 copy-done.4
  93.7 1.3 copy-done.6
  95.0 1.1 copy-done.14
  96.1 0.0 collective-permute-done.2.refs_1_.inner_got
  96.1 0.0 collective-permute-done.3.refs_2_.outer_got
  96.1 11.9 %all-to-all-done.2.got_ref = bf16[32,192,128]{2,1,0:T(8,128)(2,1)S(1)} async-done(((bf16[32,192,128]{2,1,0:T(8,128)(2,1)}), bf16[32,192,128]{2,1,0:T(8,128)(2,1)S(1)}, u32[]{:S(2)}, u32[]{:S(2)}) %all-to-all-start.2) | async-done | bytes 1572896 | tf_op jit(solution)/shard_map/all_to_all | solution.py:290
  108.0 1.7 %shard_map.136 = bf16[32,192,128]{2,1,0:T(8,128)(2,1)S(1)} custom-call(s32[3,7]{1,0:T(4,128)} %offsets_ref.3, bf16[32,192,128]{2,1,0:T(8,128)(2,1)S(1)} %all-to-all-done.2.got_ref, f32[3,256,128]{2,1,0:T(8,128)S(1)} %get-tuple-element.34.refs_0_.local_ref, bf16[256,128]{1,0:T(8,128)(2,1)S(1)} %collective-permute-done.2.refs_1_.inner_got, ...), custom_call_target="tpu_custom_call" | custom-call | flops 786432 | bytes 393216 | tf_op jit(solution)/shard_map/pallas_call | solution.py:399
  109.8 0.0 copy-start.3
  109.8 0.0 copy-start.15
  109.8 28.5 %all_to_all.21.got_ref = bf16[32,192,128]{2,1,0:T(8,128)(2,1)S(1)} all-to-all(bf16[32,192,128]{2,1,0:T(8,128)(2,1)S(1)} %shard_map.136), channel_id=1, replica_groups=mesh['chan'=32,'hel'=4] {'chan'}, dimensions={0} | all-to-all | bytes 3145728 | tf_op jit(solution)/shard_map/all_to_all | solution.py:290
  138.3 0.0 copy-done.3
  138.3 0.0 copy-done.15
  138.3 3.3 %shard_map.137 = f32[3,128,256]{2,1,0:T(8,128)} custom-call(s32[3]{0:T(128)} %counts_ref.9, f32[8,256,128]{2,1,0:T(8,128)S(1)} %copy-done.15, f32[256,128]{1,0:T(8,128)S(1)} %copy-done.1, f32[256,128]{1,0:T(8,128)S(1)} %copy-done, f32[3,128]{1,0:T(4,128)S(1)} %copy-done.20, bf16[32,192,128]{2,1,0:T(8,128)(2,1)S(1)} %all_to_all.21.got_ref, ...), custom_call_target="tpu_custom_call" | custom-call | flops 1409286144 | bytes 3145728 | tf_op jit(solution)/shard_map/pallas_call | solution.py:402
  (25 shorter events, 0.0 us)
Async XLA Ops:
  7.2 11.0 %copy-start.25 = (bf16[256,128]{1,0:T(8,128)(2,1)S(1)}, bf16[256,128]{1,0:T(8,128)(2,1)}, u32[]{:S(2)}) copy-start(bf16[256,128]{1,0:T(8,128)(2,1)} %get-tuple-element.25) | copy-start | bytes 196612
  7.3 11.1 %copy-start.24 = (bf16[256,128]{1,0:T(8,128)(2,1)S(1)}, bf16[256,128]{1,0:T(8,128)(2,1)}, u32[]{:S(2)}) copy-start(bf16[256,128]{1,0:T(8,128)(2,1)} %get-tuple-element.26) | copy-start | bytes 196612
  7.3 11.7 %copy-start = (f32[256,128]{1,0:T(8,128)S(1)}, f32[256,128]{1,0:T(8,128)}, u32[]{:S(2)}) copy-start(f32[256,128]{1,0:T(8,128)} %constant.8.clone.damp_ref) | copy-start | bytes 393220
  7.3 11.7 %copy-start.1 = (f32[256,128]{1,0:T(8,128)S(1)}, f32[256,128]{1,0:T(8,128)}, u32[]{:S(2)}) copy-start(f32[256,128]{1,0:T(8,128)} %constant.7.clone.cent_ref) | copy-start | bytes 393220
  7.3 11.7 %copy-start.18 = (f32[256,256]{1,0:T(8,128)S(1)}, f32[256,256]{1,0:T(8,128)}, u32[]{:S(2)}) copy-start(f32[256,256]{1,0:T(8,128)} %constant.6.clone.kin_ref) | copy-start | bytes 786436
  7.3 11.7 %copy-start.19 = (f32[8,256]{1,0:T(8,128)S(1)}, f32[8,256]{1,0:T(8,128)}, u32[]{:S(2)}) copy-start(f32[8,256]{1,0:T(8,128)} %radial_ref.3) | copy-start | bytes 24580
  7.3 11.7 %copy-start.20 = (f32[3,128]{1,0:T(4,128)S(1)}, f32[3,128]{1,0:T(4,128)}, u32[]{:S(2)}) copy-start(f32[3,128]{1,0:T(4,128)} %cor_ref.7) | copy-start | bytes 4612
  7.3 11.7 %copy-start.21 = (f32[3,128]{1,0:T(4,128)S(1)}, f32[3,128]{1,0:T(4,128)}, u32[]{:S(2)}) copy-start(f32[3,128]{1,0:T(4,128)} %e_ref.3) | copy-start | bytes 4612
  7.3 11.7 %copy-start.22 = (f32[3,128]{1,0:T(4,128)S(1)}, f32[3,128]{1,0:T(4,128)}, u32[]{:S(2)}) copy-start(f32[3,128]{1,0:T(4,128)} %rot_ref.3) | copy-start | bytes 4612
  7.4 34.6 %all-to-all-start = ((bf16[32,192,128]{2,1,0:T(8,128)(2,1)}), bf16[32,192,128]{2,1,0:T(8,128)(2,1)S(1)}, u32[]{:S(2)}, u32[]{:S(2)}) async-start(bf16[32,192,128]{2,1,0:T(8,128)(2,1)} %get-tuple-element.23), calls=%async_computation | async-start | bytes 3145728 | tf_op jit(solution)/shard_map/all_to_all | solution.py:290
  18.2 10.8 %collective-permute-start = (bf16[256,128]{1,0:T(8,128)(2,1)S(1)}, bf16[256,128]{1,0:T(8,128)(2,1)S(1)}, u32[]{:S(2)}, u32[]{:S(2)}) collective-permute-start(bf16[256,128]{1,0:T(8,128)(2,1)S(1)} %copy-done.25), channel_id=1, source_target_pairs={{0,1},{2,3},{1,0},{3,2},{4,5},{6,7},{5,4},{7,6},{8,9},{10,11},{9,8... | collective-permute-start | bytes 196616 | tf_op jit(solution)/shard_map/ppermute | solution.py:286
  18.3 10.7 %collective-permute-start.1 = (bf16[256,128]{1,0:T(8,128)(2,1)S(1)}, bf16[256,128]{1,0:T(8,128)(2,1)S(1)}, u32[]{:S(2)}, u32[]{:S(2)}) collective-permute-start(bf16[256,128]{1,0:T(8,128)(2,1)S(1)} %copy-done.24), channel_id=1, source_target_pairs={{1,2},{2,1},{5,6},{6,5},{9,10},{10,9},{13,14},{14,13},{17,18},{18,... | collective-permute-start | bytes 196616 | tf_op jit(solution)/shard_map/ppermute | solution.py:286
  24.3 1.2 copy-start.8
  25.5 1.2 copy-start.10
  26.7 1.3 copy-start.12
  28.0 1.1 copy-start.16
  42.0 31.4 %copy-start.11 = (bf16[7,8,128,128]{3,2,1,0:T(8,128)(2,1)S(1)}, bf16[7,8,128,128]{3,2,1,0:T(8,128)(2,1)}, u32[]{:S(2)}) copy-start(bf16[7,8,128,128]{3,2,1,0:T(8,128)(2,1)} %copy-done.10) | copy-start | bytes 5505028
  42.0 31.4 %copy-start.13 = (bf16[7,8,128,128]{3,2,1,0:T(8,128)(2,1)S(1)}, bf16[7,8,128,128]{3,2,1,0:T(8,128)(2,1)}, u32[]{:S(2)}) copy-start(bf16[7,8,128,128]{3,2,1,0:T(8,128)(2,1)} %copy-done.12) | copy-start | bytes 5505028
  43.7 29.7 %copy-start.9 = (bf16[7,8,128,128]{3,2,1,0:T(8,128)(2,1)S(1)}, bf16[7,8,128,128]{3,2,1,0:T(8,128)(2,1)}, u32[]{:S(2)}) copy-start(bf16[7,8,128,128]{3,2,1,0:T(8,128)(2,1)} %copy-done.8) | copy-start | bytes 5505028
  43.7 29.7 %copy-start.17 = (f32[8,256,128]{2,1,0:T(8,128)S(1)}, f32[8,256,128]{2,1,0:T(8,128)}, u32[]{:S(2)}) copy-start(f32[8,256,128]{2,1,0:T(8,128)} %copy-done.16) | copy-start | bytes 3145732
  79.1 5.0 %copy-start.23 = (bf16[256,128]{1,0:T(8,128)(2,1)S(1)}, bf16[256,128]{1,0:T(8,128)(2,1)}, u32[]{:S(2)}) copy-start(bf16[256,128]{1,0:T(8,128)(2,1)} %get-tuple-element.36) | copy-start | bytes 196612
  79.1 28.9 %all-to-all-start.2 = ((bf16[32,192,128]{2,1,0:T(8,128)(2,1)}), bf16[32,192,128]{2,1,0:T(8,128)(2,1)S(1)}, u32[]{:S(2)}, u32[]{:S(2)}) async-start(bf16[32,192,128]{2,1,0:T(8,128)(2,1)} %get-tuple-element.33), calls=%async_computation.2 | async-start | bytes 3145728 | tf_op jit(solution)/shard_map/all_to_all | solution.py:290
  84.0 12.1 %collective-permute-start.2 = (bf16[256,128]{1,0:T(8,128)(2,1)}, bf16[256,128]{1,0:T(8,128)(2,1)S(1)}, u32[]{:S(2)}, u32[]{:S(2)}) collective-permute-start(bf16[256,128]{1,0:T(8,128)(2,1)} %get-tuple-element.35), channel_id=1, source_target_pairs={{0,1},{2,3},{1,0},{3,2},{4,5},{6,7},{5,4},{7,6},{8,9},{10,11},{9,8... | collective-permute-start | bytes 196616 | tf_op jit(solution)/shard_map/ppermute | solution.py:286
  84.1 12.0 %collective-permute-start.3 = (bf16[256,128]{1,0:T(8,128)(2,1)S(1)}, bf16[256,128]{1,0:T(8,128)(2,1)S(1)}, u32[]{:S(2)}, u32[]{:S(2)}) collective-permute-start(bf16[256,128]{1,0:T(8,128)(2,1)S(1)} %copy-done.23), channel_id=1, source_target_pairs={{1,2},{2,1},{5,6},{6,5},{9,10},{10,9},{13,14},{14,13},{17,18},{18,... | collective-permute-start | bytes 196616 | tf_op jit(solution)/shard_map/ppermute | solution.py:286
  91.3 1.2 copy-start.2
  92.5 1.2 copy-start.4
  93.7 1.3 copy-start.6
  95.0 1.1 copy-start.14
  108.0 30.3 %copy-start.5 = (bf16[7,8,128,128]{3,2,1,0:T(8,128)(2,1)S(1)}, bf16[7,8,128,128]{3,2,1,0:T(8,128)(2,1)}, u32[]{:S(2)}) copy-start(bf16[7,8,128,128]{3,2,1,0:T(8,128)(2,1)} %copy-done.4) | copy-start | bytes 5505028
  108.0 30.3 %copy-start.7 = (bf16[7,8,128,128]{3,2,1,0:T(8,128)(2,1)S(1)}, bf16[7,8,128,128]{3,2,1,0:T(8,128)(2,1)}, u32[]{:S(2)}) copy-start(bf16[7,8,128,128]{3,2,1,0:T(8,128)(2,1)} %copy-done.6) | copy-start | bytes 5505028
  109.8 28.5 %copy-start.3 = (bf16[7,8,128,128]{3,2,1,0:T(8,128)(2,1)S(1)}, bf16[7,8,128,128]{3,2,1,0:T(8,128)(2,1)}, u32[]{:S(2)}) copy-start(bf16[7,8,128,128]{3,2,1,0:T(8,128)(2,1)} %copy-done.2) | copy-start | bytes 5505028
  109.8 28.5 %copy-start.15 = (f32[8,256,128]{2,1,0:T(8,128)S(1)}, f32[8,256,128]{2,1,0:T(8,128)}, u32[]{:S(2)}) copy-start(f32[8,256,128]{2,1,0:T(8,128)} %copy-done.14) | copy-start | bytes 3145732
